TPU v7x, 256 devices: a whole 4x4x8 slice. The times are simulated.
256 devices in a mesh: tm: 4 (over x), space: 64 (over z, y, core).
Axes of the slice: x: 4, y: 4, z: 8, core: 2. Of those that a mesh axis runs over, the one named last changes fastest.
Arguments:
- embeddings: bfloat16 [8, 131072, 128], P('tm', 'space'), may hold values from -8 to 8
- class_blocks: int32 [4, 64, 19, 8], P('tm', 'space'), may hold values from 0 to 31, as said below
- class_counts: int32 [4, 64, 19], P('tm', 'space'), may hold values from 0 to 8, as said below
- means: float32 [19, 5, 128], replicated, may hold values from -3 to 3
- log_weights: float32 [19, 5], replicated, may hold values from -21 to 1
- factors: bfloat16 [19, 5, 128, 128], replicated, may hold values from -1 to 4, as said below
Outputs:
- new_log_weights: float32 [19, 5], replicated
- new_means: float32 [19, 5, 128], replicated
- new_factors: float32 [19, 5, 128, 128], replicated
Inputs may be any that keep to these rules, and one draw needn't show every extreme that they name: `class_blocks`: on each device, every class list names distinct local blocks and no block is named in two lists; entries beyond a list's count are arbitrary block indices. `class_counts`: on every device one class has exactly 8 blocks; on one device every block belongs to some class. `factors`: each factor is upper triangular with a positive diagonal.
All inputs are finite; a program needn't handle non-finite values.
Results may differ from a plain program's by a relative error of at most 0.0003.
Values sent between devices are 32-bit elements; how exact they have to be, the bound alone decides.
No kernel may reach another device: no remote copies, remote signals or barrier semaphores. Data moves between devices by JAX's collectives and lax.ppermute only.
A program may use at most 192 MiB of HBM per device.

v0:
```python
import jax
import jax.numpy as jnp
from jax import lax
from jax.sharding import PartitionSpec as P

BLOCK = 128


prior_weight = 1.0
prior_spread = 1.0
highest = lax.Precision.HIGHEST


def block_stats(block_rows, block_class, block_live, factors, mean_proj, log_const):
    gathered = factors[block_class]
    projected = jnp.einsum(
        "bpi,bkij->bpkj", block_rows, gathered, preferred_element_type=jnp.float32
    )
    centred = projected - mean_proj[block_class][:, None, :, :]
    scores = log_const[block_class][:, None, :] - 0.5 * jnp.sum(centred * centred, axis=-1)
    weights = jax.nn.softmax(scores, axis=-1) * block_live[:, None, None]
    rows_float = block_rows.astype(jnp.float32)
    counts = jnp.sum(weights, axis=1)
    totals = jnp.einsum("bpk,bpi->bki", weights, rows_float, precision=highest)
    weighted = weights[:, :, :, None] * rows_float[:, :, None, :]
    second = jnp.einsum("bpki,bpj->bkij", weighted, rows_float, precision=highest)
    return (counts, totals, second)


def class_members(class_lists, list_counts, block_total):
    positions = jnp.arange(class_lists.shape[1], dtype=jnp.int32)
    member = (
        class_lists[:, :, None] == jnp.arange(block_total, dtype=jnp.int32)[None, None, :]
    ) & (positions[None, :, None] < list_counts[:, None, None])
    present = jnp.any(member, axis=1)
    class_ids = jnp.arange(class_lists.shape[0], dtype=jnp.int32)
    block_class = jnp.sum(jnp.where(present, class_ids[:, None], 0), axis=0)
    onehot = present.astype(jnp.float32)
    return (onehot, block_class, jnp.sum(onehot, axis=0))


def class_reduce(onehot, counts, totals, second):
    return (
        jnp.einsum("cb,bk->ck", onehot, counts, precision=highest),
        jnp.einsum("cb,bki->cki", onehot, totals, precision=highest),
        jnp.einsum("cb,bkij->ckij", onehot, second, precision=highest),
    )


def update(counts, totals, second, mean_old):
    width = totals.shape[-1]
    denom = counts + prior_weight
    new_mean = (totals + prior_weight * mean_old) / denom[:, None]
    scatter = (
        second
        + prior_weight * mean_old[:, :, None] * mean_old[:, None, :]
        - denom[:, None, None] * new_mean[:, :, None] * new_mean[:, None, :]
    )
    identity = jnp.eye(width, dtype=jnp.float32)
    covariance = (scatter + prior_spread * identity) / denom[:, None, None]
    lower_factor = jnp.linalg.cholesky(covariance)
    inverse = jax.scipy.linalg.solve_triangular(
        lower_factor, jnp.broadcast_to(identity, covariance.shape), lower=True
    )
    return (new_mean, jnp.swapaxes(inverse, 1, 2))


def pack_pairs(pair_counts, pair_totals, pair_second, padded):
    extra = padded - pair_counts.shape[0]
    width = pair_totals.shape[-1]
    pair_counts = jnp.pad(pair_counts, (0, extra))
    pair_totals = jnp.pad(pair_totals, ((0, extra), (0, 0)))
    pair_second = jnp.pad(pair_second, ((0, extra), (0, 0), (0, 0)))
    half_count = padded // 2
    lower_mask = jnp.tril(jnp.ones((width, width), dtype=bool))
    folded = jnp.where(lower_mask, pair_second[:half_count], pair_second[half_count:])
    upper_diag = jnp.diagonal(pair_second[half_count:], axis1=1, axis2=2)
    both_counts = jnp.stack([pair_counts[:half_count], pair_counts[half_count:]], axis=1)
    both_totals = jnp.stack([pair_totals[:half_count], pair_totals[half_count:]], axis=1)
    return (both_counts, both_totals, folded, upper_diag)


def unpack_pairs(folded, upper_diag):
    width = folded.shape[-1]
    identity = jnp.eye(width, dtype=jnp.float32)
    strict_lower = jnp.tril(jnp.ones((width, width), dtype=bool), -1)
    strict_upper = jnp.transpose(strict_lower)
    lower_part = jnp.where(strict_lower, folded, 0.0)
    diag_first = jnp.diagonal(folded, axis1=1, axis2=2)
    second_first = lower_part + jnp.swapaxes(lower_part, 1, 2) + diag_first[:, :, None] * identity
    upper_part = jnp.where(strict_upper, folded, 0.0)
    second_later = upper_part + jnp.swapaxes(upper_part, 1, 2) + upper_diag[:, :, None] * identity
    return (second_first, second_later)


def solve_share(share_counts, share_totals, share_folded, share_diag, mean_first, mean_later):
    width = share_totals.shape[-1]
    second_first, second_later = unpack_pairs(share_folded, share_diag)
    new_first, factor_first = update(
        share_counts[:, 0], share_totals[:, 0], second_first, mean_first
    )
    new_later, factor_later = update(
        share_counts[:, 1], share_totals[:, 1], second_later, mean_later
    )
    strict_lower = jnp.tril(jnp.ones((width, width), dtype=bool), -1)
    folded_factor = jnp.where(strict_lower, jnp.swapaxes(factor_later, 1, 2), factor_first)
    later_diag = jnp.diagonal(factor_later, axis1=1, axis2=2)
    return (jnp.stack([new_first, new_later], axis=1), folded_factor, later_diag)


def unfold_factors(folded_factor, later_diag):
    width = folded_factor.shape[-1]
    identity = jnp.eye(width, dtype=jnp.float32)
    upper_mask = jnp.triu(jnp.ones((width, width), dtype=bool))
    strict_lower = jnp.tril(jnp.ones((width, width), dtype=bool), -1)
    factor_first = jnp.where(upper_mask, folded_factor, 0.0)
    factor_later = (
        jnp.swapaxes(jnp.where(strict_lower, folded_factor, 0.0), 1, 2)
        + later_diag[:, :, None] * identity
    )
    return (factor_first, factor_later)


def body(embeddings, class_blocks, class_counts, means, log_weights, factors):
    frames_here, pixels_here, width = embeddings.shape
    block_total = frames_here * pixels_here // BLOCK
    block_rows = embeddings.reshape(block_total, BLOCK, width)
    num_classes, num_comps, _ = means.shape
    class_lists = class_blocks[0, 0]
    list_counts = class_counts[0, 0]
    factors_float = factors.astype(jnp.float32)
    mean_proj = jnp.einsum("cki,ckij->ckj", means, factors_float, precision=highest)
    log_const = log_weights + jnp.sum(
        jnp.log(jnp.diagonal(factors_float, axis1=2, axis2=3)), axis=-1
    )
    onehot, block_class, block_live = class_members(class_lists, list_counts, block_total)
    terms = block_stats(block_rows, block_class, block_live, factors, mean_proj, log_const)
    counts_c, totals_c, second_c = class_reduce(onehot, *terms)
    pair_count = num_classes * num_comps
    counts_p = counts_c.reshape(pair_count)
    totals_p = totals_c.reshape(pair_count, width)
    second_p = second_c.reshape(pair_count, width, width)
    mean_old = means.reshape(pair_count, width)
    space_total = lax.axis_size("space")
    padded = 2 * space_total * ((pair_count + 2 * space_total - 1) // (2 * space_total))
    half_count = padded // 2
    packed = pack_pairs(counts_p, totals_p, second_p, padded)
    scattered = (
        lax.psum_scatter(packed[0], "space", scatter_dimension=0, tiled=True),
        lax.psum_scatter(packed[1], "space", scatter_dimension=0, tiled=True),
        lax.psum_scatter(packed[2], "space", scatter_dimension=0, tiled=True),
        lax.psum_scatter(packed[3], "space", scatter_dimension=0, tiled=True),
    )
    share_counts, share_totals, share_folded, share_diag = lax.psum(
        (scattered[0], scattered[1], scattered[2], scattered[3]), "tm"
    )
    share_rows = half_count // space_total
    first_row = lax.axis_index("space") * share_rows
    mean_padded = jnp.pad(mean_old, ((0, padded - pair_count), (0, 0)))
    mean_first = lax.dynamic_slice_in_dim(mean_padded, first_row, share_rows)
    mean_later = lax.dynamic_slice_in_dim(mean_padded, half_count + first_row, share_rows)
    share_means, folded_factor, later_diag = solve_share(
        share_counts, share_totals, share_folded, share_diag, mean_first, mean_later
    )
    gathered_means, gathered_folded, gathered_diag, gathered_counts = (
        lax.all_gather(share_means, "space", axis=0, tiled=True),
        lax.all_gather(folded_factor, "space", axis=0, tiled=True),
        lax.all_gather(later_diag, "space", axis=0, tiled=True),
        lax.all_gather(share_counts, "space", axis=0, tiled=True),
    )
    factor_first, factor_later = unfold_factors(gathered_folded, gathered_diag)
    new_mean = jnp.concatenate([gathered_means[:, 0], gathered_means[:, 1]])[:pair_count]
    new_factor = jnp.concatenate([factor_first, factor_later])[:pair_count]
    counts_all = jnp.concatenate([gathered_counts[:, 0], gathered_counts[:, 1]])[:pair_count]
    counts_grid = counts_all.reshape(num_classes, num_comps)
    new_log = jnp.log(counts_grid + 1.0) - jnp.log(
        jnp.sum(counts_grid, axis=1, keepdims=True) + num_comps
    )
    return (
        new_log,
        new_mean.reshape(num_classes, num_comps, width),
        new_factor.reshape(num_classes, num_comps, width, width),
    )


def solution(mesh):
    return jax.shard_map(
        body,
        mesh=mesh,
        in_specs=(
            P("tm", "space", None),
            P("tm", "space", None, None),
            P("tm", "space", None),
            P(),
            P(),
            P(),
        ),
        out_specs=(P(), P(), P()),
        check_vma=False,
    )
```

profile of v0, /device:TPU:1, one launch (start us, length us, event | category | flops | bytes accessed | tf_op | source)
XLA Modules:
  0.0 623.0 jit_solution(16386797436783175942)
XLA Ops:
  8.9 24.0 %copy.154 = f32[19,5,128,128]{0,1,3,2:T(8,128)} copy(bf16[19,5,128,128]{3,2,1,0:T(8,128)(2,1)} %param.14) | data formatting | bytes 9338880 | tf_op jit(solution)/shard_map/convert_element_type | solution.py:131
  32.9 3.6 gather_fusion.2
  42.3 6.8 %multiply_reduce_fusion = f32[32,5,128]{2,1,0:T(8,128)S(1)} fusion(f32[32,5,128]{2,1,0:T(8,128)S(1)} %gather_fusion.3, bf16[32,5,128,128]{3,2,1,0:T(8,128)(2,1)} %gather_fusion.2, bf16[32,128,128,1]{2,1,3,0:T(8,128)(2,1)} %bitcast.136), kind=kOutput, calls=%fused_computation.12 | convolution fusion | flops 678932480 | bytes 6455296 | tf_op jit(solution)/shard_map/bpi,bkij->bpkj/dot_general | solution.py:16
  49.1 3.2 fusion.45
  55.2 5.7 fusion.3
  60.9 11.2 %fusion.1 = f32[19,5,128,128]{3,0,2,1:T(8,128)S(1)} fusion(f32[32,5,128,128]{3,2,1,0:T(8,128)S(1)} %fusion.3, pred[19,32]{1,0:T(8,128)(4,1)S(1)} %fusion.15), kind=kOutput, calls=%fused_computation.8 | convolution fusion | flops 597688320 | bytes 16712288 | tf_op jit(solution)/shard_map/cb,bkij->ckij/dot_general | solution.py:46
  72.1 3.8 copy.166
  75.9 8.5 %copy.167 = f32[95,128,128]{0,2,1:T(8,128)} copy(f32[95,128,128]{2,1,0:T(8,128)} %bitcast.134) | data formatting | bytes 12451840 | tf_op jit(solution)/shard_map/reshape | solution.py:142
  84.4 17.0 %slice_select_fusion = (f32[64,128,128]{0,2,1:T(8,128)}, f32[64,128,128]{0,2,1:T(8,128)}) fusion(f32[95,128,128]{0,2,1:T(8,128)} %copy.167, pred[128,128]{1,0:T(8,128)(4,1)S(1)} %iota_compare_fusion.7), kind=kLoop, calls=%fused_computation.13 | loop fusion | flops 1048576 | bytes 25182208 | tf_op jit(solution)/shard_map/jit(_where)/select_n | solution.py:76
  101.4 7.3 %copy.169 = f32[64,128,128]{2,1,0:T(8,128)} copy(f32[64,128,128]{0,2,1:T(8,128)} %get-tuple-element.36) | data formatting | bytes 8388608 | tf_op jit(solution)/shard_map/jit(_where)/select_n | solution.py:76
  111.5 250.2 %all-reduce.8 = (f32[64,2]{0,1:T(2,128)S(1)}, f32[64,128]{0,1:T(8,128)S(1)}) all-reduce(f32[64,2]{0,1:T(2,128)S(1)} %pad_maximum_fusion.3, f32[64,128]{0,1:T(8,128)S(1)} %bitcast.144), channel_id=3, replica_groups=mesh['tm'=4,'space'=64] {'space'}, use_global_device_ids=true, to_apply=%region_8.9.clone | all-reduce | flops 8320 | bytes 66560
  364.6 8.7 %all-reduce.9 = (f32[1,2]{0,1:T(2,128)S(1)}, f32[1,2,128]{2,1,0:T(2,128)S(1)}, f32[128]{0:T(128)S(1)}) all-reduce(f32[1,2]{0,1:T(2,128)S(1)} %constant_dynamic-slice_fusion.1, f32[1,2,128]{2,1,0:T(2,128)S(1)} %constant_dynamic-slice_fusion, f32[128]{0:T(128)S(1)} %dynamic-slice_reduce_fusion), channel_id=1, replica_groups=mesh['tm'=4,'space'=64] {'tm'}, use_global_device_ids=true, to_apply=%region_9.10 | all-reduce | flops 386 | bytes 3088 | tf_op jit(solution)/shard_map/psum | solution.py:154
  375.5 42.8 %all-reduce.13.cloned.1.call-done = f32[1,128,128]{2,1,0:T(8,128)} async-done(((f32[1,128,128]{2,1,0:T(8,128)}), f32[1,128,128]{2,1,0:T(8,128)}) %all-reduce.13.cloned.1.call-update) | async-done | bytes 65552 | tf_op jit(solution)/shard_map/psum | solution.py:154
  419.7 11.7 %custom-call.16 = f32[1,128,128]{2,1,0:T(8,128)S(1)} custom-call(f32[1,128,128]{2,1,0:T(8,128)S(1)} %fusion.24), custom_call_target="Cholesky" | custom-call | tf_op jit(solution)/shard_map/jit(cholesky)/cholesky | solution.py:61
  432.8 9.8 %custom-call.17 = f32[1,128,128]{1,2,0:T(8,128)S(1)} custom-call(f32[1,128,128]{2,1,0:T(8,128)S(1)} %select_select_fusion.1), custom_call_target="InvertDiagBlocksLowerTriangular" | custom-call | tf_op jit(solution)/shard_map/jit(_solve_triangular)/triangular_solve | solution.py:62
  445.1 11.7 %custom-call.18 = f32[1,128,128]{2,1,0:T(8,128)S(1)} custom-call(f32[1,128,128]{2,1,0:T(8,128)S(1)} %fusion.19), custom_call_target="Cholesky" | custom-call | tf_op jit(solution)/shard_map/jit(cholesky)/cholesky | solution.py:61
  458.2 10.0 %custom-call.19 = f32[1,128,128]{1,2,0:T(8,128)S(1)} custom-call(f32[1,128,128]{2,1,0:T(8,128)S(1)} %select_select_fusion), custom_call_target="InvertDiagBlocksLowerTriangular" | custom-call | tf_op jit(solution)/shard_map/jit(_solve_triangular)/triangular_solve | solution.py:62
  469.2 47.2 %all_gather.13 = f32[64,2,128]{2,1,0:T(2,128)S(1)} all-gather(f32[1,2,128]{2,1,0:T(2,128)S(1)} %pad_maximum_fusion.4), channel_id=1, replica_groups=mesh['tm'=4,'space'=64] {'space'}, dimensions={0}, use_global_device_ids=true | all-gather | bytes 66560 | tf_op jit(solution)/shard_map/all_gather | solution.py:166
  517.3 37.8 %all-gather.1 = f32[64,1,2]{2,1,0:T(1,128)S(1)} all-gather(f32[1,1,2]{2,1,0:T(1,128)S(1)} %bitcast.158), channel_id=1, replica_groups=mesh['tm'=4,'space'=64] {'space'}, dimensions={0}, use_global_device_ids=true | all-gather | bytes 520 | tf_op jit(solution)/shard_map/all_gather | solution.py:169
  557.5 37.8 %all-gather.2 = f32[64,1,128]{2,1,0:T(1,128)S(1)} all-gather(f32[1,1,128]{2,1,0:T(1,128)S(1)} %bitcast.159), channel_id=2, replica_groups=mesh['tm'=4,'space'=64] {'space'}, dimensions={0}, use_global_device_ids=true | all-gather | bytes 33280 | tf_op jit(solution)/shard_map/all_gather | solution.py:168
  595.3 5.6 copy.178
  600.9 2.8 broadcast_select_fusion
  604.9 3.4 pad_maximum_fusion
  608.3 7.9 %copy.183 = f32[19,5,128,128]{3,2,1,0:T(8,128)} copy(f32[19,5,128,128]{2,3,1,0:T(8,128)} %bitcast.135) | data formatting | bytes 12451840
  (102 shorter events, 28.9 us)
Async XLA Ops:
  7.2 356.1 %all-reduce.15.cloned.1.call-start = ((), (), s32[]{:S(2)}) async-start(), calls=%async_computation.3 | async-start | bytes 131072
  8.9 24.0 %copy-start = (bf16[19,5,128,128]{3,2,1,0:T(8,128)(2,1)S(1)}, bf16[19,5,128,128]{3,2,1,0:T(8,128)(2,1)}, u32[]{:S(2)}) copy-start(bf16[19,5,128,128]{3,2,1,0:T(8,128)(2,1)} %param.14) | copy-start | bytes 9338884
  32.9 3.6 copy-start.3
  32.9 8.7 %copy-start.4 = (f32[19,5]{0,1:T(8,128)S(1)}, f32[19,5]{0,1:T(8,128)}, u32[]{:S(2)}) copy-start(f32[19,5]{0,1:T(8,128)} %param.13) | copy-start | bytes 1144
  42.3 10.2 %copy-start.2 = (bf16[2,2048,128]{2,1,0:T(8,128)(2,1)S(1)}, bf16[2,2048,128]{2,1,0:T(8,128)(2,1)}, u32[]{:S(2)}) copy-start(bf16[2,2048,128]{2,1,0:T(8,128)(2,1)} %param.9) | copy-start | bytes 3145732
  54.3 320.9 %reduce-scatter.6.cloned.1.call-start = ((), (), s32[]{:S(2)}) async-start(), calls=%async_computation.4 | async-start | bytes 4259840
  101.4 9.5 %copy-start.5 = (u32[256]{0:T(256)S(1)}, u32[256]{0:T(256)}, u32[]{:S(2)}) copy-start(u32[256]{0:T(256)} %constant.164) | copy-start | bytes 3076
  108.7 309.5 %all-reduce.13.cloned.1.call-start = ((), (), s32[]{:S(2)}) async-start(), calls=%async_computation.1 | async-start | bytes 131072 | tf_op jit(solution)/shard_map/psum | solution.py:154
  375.2 220.1 %all-gather.5.cloned.1.call-start = ((), (), s32[]{:S(2)}) async-start(), calls=%async_computation.2 | async-start | bytes 4259840 | tf_op jit(solution)/shard_map/all_gather | solution.py:167
  600.9 3.4 copy-start.1
Sparse Core Ops, SparseCore 0:
  54.4 171.9 all-reduce.14
  231.1 135.7 reduce-scatter.5
  375.3 42.8 all-reduce.12
  469.2 81.9 all-gather.4
where the time goes:
time: 630 us; the launch traced here: 623 us
  blocking collectives  382 us (61%)
  local copies, waits for them, and re-layouts  78 us (12%)
  other arithmetic  75.9 us (12%)
  waiting for transfers between devices  42.9 us (7%)
  matrix products  28.5 us (5%)
  between operations  15.8 us (3%)
    unnamed x1, blocking collectives  250 us
    all_gather x1, blocking collectives, body(): lax.all_gather(share_means, 'space', axis=0, tiled=True)  47.2 us
    psum x1, waiting for transfers between devices, body(): lax.psum((scattered[0], scattered[1], scattered[2], scattered[3]), 'tm')  42.8 us
    all_gather x1, blocking collectives, body(): lax.all_gather(share_counts, 'space', axis=0, tiled=True)  37.8 us
    all_gather x1, blocking collectives, body(): lax.all_gather(later_diag, 'space', axis=0, tiled=True)  37.8 us
    another operation x6, other arithmetic, update(): lower_factor = jnp.linalg.cholesky(covariance)  24.8 us
    convert_element_type x1, local copies, waits for them, and re-layouts, body(): factors_float = factors.astype(jnp.float32)  24 us
    another operation x4, other arithmetic, update(): jax.scipy.linalg.solve_triangular(lower_factor, jnp.broadcast_to(identity...  21.1 us
  transfers between devices with their start and end apart: 4, of which 1 were waited for; matrix products, arithmetic and copies ran while one was open for 10% of the time, Pallas kernels for 0%

commit v1 on v0

v1 whole, which is shorter than its diff:
```python
import functools
import jax
import jax.numpy as jnp
from jax import lax
from jax.experimental import pallas as pl
from jax.experimental.pallas import tpu as pltpu
from jax.sharding import Mesh, PartitionSpec as P

CLASSES = 19
COMPS = 5
WIDTH = 128
BLOCK = 128
ROWS = 72
STRIPS = 16
F32 = jnp.float32
BF16 = jnp.bfloat16
SLOTS = 96
HALF = 48
VMEM_LIMIT = 48 * 1024 * 1024


def iota(shape, axis):
    return lax.broadcasted_iota(jnp.int32, shape, axis)


def pieces(value, count):
    out = []
    for _ in range(count):
        part = value.astype(BF16)
        out.append(part)
        value = value - part.astype(F32)
    return out


def pack_strips(strips, extra):
    lane = iota((8, WIDTH), 1)
    out = [strips[0]]
    for s in range(1, 8):
        moved = pltpu.roll(strips[16 - s], 8 * s, 1)
        out.append(jnp.where(lane >= 8 * s, strips[s], moved))
    out.append(jnp.where(lane >= 64, strips[8], extra))
    return out


def unpack_strips(slots):
    lane = iota((8, WIDTH), 1)
    strips = [None] * 16
    strips[0] = slots[0]
    for s in range(1, 8):
        strips[s] = jnp.where(lane >= 8 * s, slots[s], 0.0)
        moved = pltpu.roll(slots[s], WIDTH - 8 * s, 1)
        strips[16 - s] = jnp.where(lane >= WIDTH - 8 * s, moved, 0.0)
    strips[8] = jnp.where(lane >= 64, slots[8], 0.0)
    return strips


def extra_rows(row, count):
    sub = iota((8, WIDTH), 0)
    later = pltpu.roll(jnp.broadcast_to(row, (8, WIDTH)), 64, 1)
    return jnp.where(sub == 0, row, jnp.where(sub == 1, later, jnp.where(sub == 2, count, 0.0)))


def split_extra(slot):
    lane = iota((8, WIDTH), 1)
    moved = pltpu.roll(slot, 64, 1)
    row = jnp.where(lane[0:1] < 64, slot[0:1], moved[1:2])
    count = jnp.where(lane[0:1] < 64, slot[2:3], moved[2:3])
    return row, count


def moments_kernel(lists, list_counts, core, lw_ref, emb_ref, fac_ref, mean_ref, own_ref, other_ref, acc, tot, cnt):
    c = pl.program_id(0)
    n = list_counts[c]
    acc[...] = jnp.zeros_like(acc)
    tot[...] = jnp.zeros_like(tot)
    cnt[...] = jnp.zeros_like(cnt)

    @pl.when(n > 0)
    def _():
        eye = iota((WIDTH, WIDTH), 0) == iota((WIDTH, WIDTH), 1)
        sub = iota((8, WIDTH), 0)
        mean = mean_ref[0]
        mean_pieces = jnp.concatenate(
            pieces(jnp.concatenate([mean, jnp.zeros((16 - COMPS, WIDTH), F32)]), 3)
        )
        diag = jnp.ones((8, WIDTH), F32)
        lw = jnp.full((8, WIDTH), -1e30, F32)
        mean_proj = []
        for k in range(COMPS):
            factor = fac_ref[0, k]
            diag_row = jnp.sum(jnp.where(eye, factor.astype(F32), 0.0), axis=0, keepdims=True)
            diag = jnp.where(sub == k, diag_row, diag)
            lw = jnp.where(sub == k, lw_ref[c, k], lw)
            parts = jnp.dot(mean_pieces, factor, preferred_element_type=F32)
            mean_proj.append(parts[k : k + 1] + parts[16 + k : 17 + k] + parts[32 + k : 33 + k])
        log_const = lw[:, 0:1] + jnp.sum(jnp.log(diag), axis=1, keepdims=True)
        selector = jnp.where(
            (iota((16, COMPS * WIDTH), 1) // WIDTH) == iota((16, COMPS * WIDTH), 0), 1.0, 0.0
        ).astype(BF16)

        def step(t, carry):
            first = emb_ref[lists[c, 2 * t]]
            later = emb_ref[lists[c, 2 * t + 1]]
            rows = jnp.concatenate([first, later], axis=0)
            rows_t = jnp.concatenate([first.astype(F32).T, later.astype(F32).T], axis=1)
            squares = []
            for k in range(COMPS):
                centred = jnp.dot(rows, fac_ref[0, k], preferred_element_type=F32) - mean_proj[k]
                squares.append(centred * centred)
            square = jnp.concatenate(squares, axis=1)
            total = None
            for part in pieces(square, 3):
                term = lax.dot_general(
                    selector, part, (((1,), (1,)), ((), ())), preferred_element_type=F32
                )
                total = term if total is None else total + term
            scores = log_const - 0.5 * total[0:8]
            top = jnp.max(scores, axis=0, keepdims=True)
            weights = jnp.exp(scores - top)
            weights = weights / jnp.sum(weights, axis=0, keepdims=True)
            live = (iota((8, 2 * BLOCK), 1) < BLOCK) | (2 * t + 1 < n)
            weights = jnp.where(live, weights, 0.0)
            both = jnp.concatenate([rows, rows], axis=0)
            for k in range(COMPS):
                scaled = rows_t * weights[k : k + 1]
                high, low = pieces(scaled, 2)
                acc[k] += jnp.dot(
                    jnp.concatenate([high, low], axis=1), both, preferred_element_type=F32
                )
            tall = jnp.concatenate([weights, jnp.zeros_like(weights)])
            sums = jnp.dot(jnp.concatenate(pieces(tall, 3)), rows, preferred_element_type=F32)
            tot[...] += sums[0:8] + sums[16:24] + sums[32:40]
            cnt[...] += weights[:, :BLOCK] + weights[:, BLOCK:]
            return carry

        lax.fori_loop(0, (n + 1) // 2, step, 0)

    count = jnp.broadcast_to(jnp.sum(cnt[...], axis=1, keepdims=True), (8, WIDTH))
    totals = tot[...]
    for k in range(COMPS):
        slots = pack_strips(
            [acc[k, 8 * s : 8 * s + 8, :] for s in range(STRIPS)],
            extra_rows(totals[k : k + 1], count[k : k + 1]),
        )
        packed = jnp.concatenate(slots, axis=0)
        slot = c * COMPS + k
        mine = (slot >= HALF) == (core[0] == 1)
        place = lax.rem(slot, HALF)

        @pl.when(mine)
        def _():
            own_ref[place] = packed

        @pl.when(jnp.logical_not(mine))
        def _():
            other_ref[place] = packed

    @pl.when(c == CLASSES - 1)
    def _():
        @pl.when(core[0] == 1)
        def _():
            own_ref[HALF - 1] = jnp.zeros((ROWS, WIDTH), F32)

        @pl.when(core[0] == 0)
        def _():
            other_ref[HALF - 1] = jnp.zeros((ROWS, WIDTH), F32)


def local_moments(blocks, lists, list_counts, core, log_weights, factors, means):
    whole = pl.BlockSpec((HALF, ROWS, WIDTH), lambda c, *_: (0, 0, 0))
    return pl.pallas_call(
        moments_kernel,
        grid_spec=pltpu.PrefetchScalarGridSpec(
            num_scalar_prefetch=3,
            grid=(CLASSES,),
            in_specs=[
                pl.BlockSpec(memory_space=pltpu.SMEM),
                pl.BlockSpec(blocks.shape, lambda c, *_: (0, 0, 0)),
                pl.BlockSpec((1, COMPS, WIDTH, WIDTH), lambda c, *_: (c, 0, 0, 0)),
                pl.BlockSpec((1, COMPS, WIDTH), lambda c, *_: (c, 0, 0)),
            ],
            out_specs=[whole, whole],
            scratch_shapes=[
                pltpu.VMEM((COMPS, WIDTH, WIDTH), F32),
                pltpu.VMEM((8, WIDTH), F32),
                pltpu.VMEM((8, WIDTH), F32),
            ],
        ),
        out_shape=[jax.ShapeDtypeStruct((HALF, ROWS, WIDTH), F32)] * 2,
        compiler_params=pltpu.CompilerParams(vmem_limit_bytes=VMEM_LIMIT),
        name="moments",
    )(lists, list_counts, core, log_weights, blocks, factors, means)


def solve_kernel(first, share_ref, mean_ref, out_ref):
    group = share_ref.shape[0]
    lane = iota((8, WIDTH), 1)
    sub = iota((8, WIDTH), 0)
    eye = iota((WIDTH, WIDTH), 0) == iota((WIDTH, WIDTH), 1)
    strips, new_means, counts = [], [], []
    for g in range(group):
        slots = [share_ref[g, 8 * s : 8 * s + 8, :] for s in range(9)]
        totals, count = split_extra(slots[8])
        old = mean_ref[pl.ds(jnp.minimum(first[0] + g, CLASSES * COMPS - 1), 1), :]
        denom = count + 1.0
        new = (totals + old) / denom
        old_t = jnp.broadcast_to(old, (WIDTH, WIDTH)).T
        new_t = jnp.broadcast_to(new * denom, (WIDTH, WIDTH)).T
        second = unpack_strips(slots)
        rows = []
        for s in range(STRIPS):
            cut = slice(8 * s, 8 * s + 8)
            scatter = second[s] + old_t[cut] * old - new_t[cut] * new
            scatter = jnp.where(lane - 8 * s == sub, scatter + 1.0, scatter)
            rows.append(jnp.where(lane >= 8 * s, scatter / denom, 0.0))
        strips.append(rows)
        new_means.append(new)
        counts.append(count)
    for s in range(STRIPS):
        for g in range(group):
            rows = strips[g]
            panel = rows[s]
            columns = [
                jnp.broadcast_to(panel[:, 8 * s + j : 8 * s + j + 1], (8, WIDTH)) for j in range(8)
            ]
            block = (lane >= 8 * s) & (lane < 8 * s + 8)
            panel = jnp.where(block, jnp.where(lane - 8 * s == sub, 1.0, 0.0), panel)
            pivots = jnp.ones((8, WIDTH), F32)
            for j in range(8):
                pivot = columns[j][j : j + 1]
                pivots = jnp.where(sub == j, pivot, pivots)
                if j < 7:
                    ratio = jnp.where(sub > j, columns[j] * (1.0 / pivot), 0.0)
                    panel = panel - ratio * panel[j : j + 1]
                    for l in range(j + 1, 8):
                        columns[l] = columns[l] - ratio * columns[l][j : j + 1]
            panel = panel * (1.0 / jnp.sqrt(pivots))
            rows[s] = panel
            if s < STRIPS - 1:
                a, b, d = [p.astype(F32) for p in pieces(panel, 3)]
                left = jnp.concatenate([a, a, b, b, a, d], axis=0).astype(BF16)
                right = jnp.concatenate([a, b, a, b, d, a], axis=0).astype(BF16)
                change = lax.dot_general(
                    left, right, (((0,), (0,)), ((), ())), preferred_element_type=F32
                )
                for t in range(s + 1, STRIPS):
                    base = jnp.where(block, 0.0, rows[t])
                    rows[t] = base - change[8 * t : 8 * t + 8]
    for g in range(group):
        lower = jnp.concatenate(
            [jnp.where(lane - 8 * s <= sub, strips[g][s], 0.0) for s in range(STRIPS)], axis=0
        )
        upper = lower.T
        slots = pack_strips(
            [upper[8 * s : 8 * s + 8] for s in range(STRIPS)],
            extra_rows(new_means[g], counts[g]),
        )
        out_ref[g] = jnp.concatenate(slots, axis=0)


def solve_share(first, share, means):
    return pl.pallas_call(
        solve_kernel,
        in_specs=[
            pl.BlockSpec(memory_space=pltpu.SMEM),
            pl.BlockSpec(memory_space=pltpu.VMEM),
            pl.BlockSpec(memory_space=pltpu.VMEM),
        ],
        out_specs=pl.BlockSpec(memory_space=pltpu.VMEM),
        out_shape=jax.ShapeDtypeStruct(share.shape, F32),
        compiler_params=pltpu.CompilerParams(vmem_limit_bytes=VMEM_LIMIT),
        name="solve",
    )(first, share, means)


def unpack_kernel(packed_ref, factor_ref, mean_ref, count_ref):
    group = packed_ref.shape[0]
    for g in range(group):
        slots = [packed_ref[g, 8 * s : 8 * s + 8, :] for s in range(9)]
        strips = unpack_strips(slots)
        for s in range(STRIPS):
            factor_ref[g, 8 * s : 8 * s + 8, :] = strips[s]
        row, count = split_extra(slots[8])
        mean_ref[0, g : g + 1, :] = row
        count_ref[0, g : g + 1, :] = count


def unpack_all(packed):
    group = 19
    steps = CLASSES * COMPS // group
    return pl.pallas_call(
        unpack_kernel,
        grid=(steps,),
        in_specs=[pl.BlockSpec((group, ROWS, WIDTH), lambda i: (i, 0, 0))],
        out_specs=[
            pl.BlockSpec((group, WIDTH, WIDTH), lambda i: (i, 0, 0)),
            pl.BlockSpec((1, group, WIDTH), lambda i: (i, 0, 0)),
            pl.BlockSpec((1, group, WIDTH), lambda i: (i, 0, 0)),
        ],
        out_shape=[
            jax.ShapeDtypeStruct((CLASSES * COMPS, WIDTH, WIDTH), F32),
            jax.ShapeDtypeStruct((steps, group, WIDTH), F32),
            jax.ShapeDtypeStruct((steps, group, WIDTH), F32),
        ],
        compiler_params=pltpu.CompilerParams(vmem_limit_bytes=VMEM_LIMIT),
        name="unpack",
    )(packed)


def spread(value, axes, count):
    return lax.all_to_all(
        jnp.broadcast_to(value[None], (count,) + value.shape), axes, 0, 0, tiled=True
    )


def body(embeddings, class_blocks, class_counts, means, log_weights, factors):
    frames_here, pixels_here, width = embeddings.shape
    blocks = embeddings.reshape(frames_here * pixels_here // BLOCK, BLOCK, width)
    core = lax.axis_index("core").astype(jnp.int32)
    own, other = local_moments(
        blocks, class_blocks[0, 0], class_counts[0, 0], core[None], log_weights, factors, means
    )
    half = own + lax.ppermute(other, "core", [(0, 1), (1, 0)])
    group = HALF // 16
    parts = lax.all_to_all(half, ("x", "y"), 0, 0, tiled=True)
    share = jnp.sum(parts.reshape(16, group, ROWS, WIDTH), axis=0)
    rows = group * ROWS // 8
    parts = lax.all_to_all(share.reshape(8, rows, WIDTH), "z", 0, 0, tiled=True)
    share = spread(jnp.sum(parts, axis=0), "z", 8).reshape(group, ROWS, WIDTH)
    place = lax.axis_index("x") * 4 + lax.axis_index("y")
    first = (core * HALF + place * group).astype(jnp.int32)
    solved = solve_share(first[None], share, means.reshape(CLASSES * COMPS, width))
    here = spread(solved, ("x", "y"), 16).reshape(HALF, ROWS, WIDTH)
    there = lax.ppermute(here, "core", [(0, 1), (1, 0)])
    packed = jnp.where(
        core == 0, jnp.concatenate([here, there]), jnp.concatenate([there, here])
    )
    new_factor, new_mean, counts = unpack_all(packed)
    counts = counts.reshape(CLASSES, COMPS, width)[:, :, 0]
    new_log = jnp.log(counts + 1.0) - jnp.log(jnp.sum(counts, axis=1, keepdims=True) + COMPS)
    return (
        new_log,
        new_mean.reshape(CLASSES, COMPS, width),
        new_factor.reshape(CLASSES, COMPS, width, width),
    )


def solution(mesh):
    wide = Mesh(mesh.devices.reshape(4, 8, 4, 2), ("x", "z", "y", "core"))
    space = ("z", "y", "core")
    return jax.shard_map(
        body,
        mesh=wide,
        in_specs=(P("x", space, None), P("x", space, None, None), P("x", space, None), P(), P(), P()),
        out_specs=(P(), P(), P()),
        check_vma=False,
    )
```

time: 630 us -> 154 us (0.24)
  blocking collectives: 382 us -> 66.5 us
  other arithmetic: 75.9 us -> 1.34 us
  local copies, waits for them, and re-layouts: 78 us -> 5.85 us
  Pallas kernels: 0 us -> 32.4 us
  starting transfers between devices: 0.33 us -> 30.8 us
  matrix products: 28.5 us -> 0 us
  waiting for transfers between devices: 42.9 us -> 14.5 us
  between operations: 15.8 us -> 0.74 us
    unnamed x1 -> x0, blocking collectives: 250 us -> none
    all_gather x3 -> x0, blocking collectives: 123 us -> none  [the longest x1 47.2 us: body(): lax.all_gather(share_means, 'space', axis=0, tiled=True)]
    all_to_all x0 -> x3, blocking collectives: none -> 66.5 us  [the longest x1 27.1 us: body(): parts = lax.all_to_all(half, ('x', 'y'), 0, 0, tiled=True)]
    another operation x13 -> x0, other arithmetic: 45.9 us -> none  [the longest x6 24.8 us: update(): lower_factor = jnp.linalg.cholesky(covariance)]
    psum x1 -> x0, waiting for transfers between devices: 42.8 us -> none  [body(): lax.psum((scattered[0], scattered[1], scattered[2], scattered[3]), 'tm')]
    pallas_call x0 -> x3, Pallas kernels: none -> 32.4 us  [the longest x1 21.9 us: local_moments(): pl.pallas_call(moments_kernel, grid_spec=pltpu.PrefetchScalarGridSpec(num...]
    ppermute x0 -> x2, starting transfers between devices: none -> 27.5 us  [the longest x1 22.1 us: body(): half = own + lax.ppermute(other, 'core', [(0, 1), (1, 0)])]
    dot_general x7 -> x0, matrix products: 27.4 us -> none  [the longest x1 11.2 us: class_reduce(): jnp.einsum('cb,bkij->ckij', onehot, second, precision=highest)]
  transfers between devices with their start and end apart: 4 -> 3, of which waited for: 1 -> 3; matrix products, arithmetic and copies ran while one was open for 10% -> 0% of each run, Pallas kernels for 0% -> 0%
where the time goes in v1:
time: 154 us; the launch traced here: 152 us
  blocking collectives  66.5 us (43%)
  Pallas kernels  32.4 us (21%)
  starting transfers between devices  30.8 us (20%)
  waiting for transfers between devices  14.5 us (9%)
  local copies, waits for them, and re-layouts  5.85 us (4%)
    all_to_all x1, blocking collectives, body(): parts = lax.all_to_all(half, ('x', 'y'), 0, 0, tiled=True)  27.1 us
    all_to_all x1, blocking collectives, spread(): lax.all_to_all(jnp.broadcast_to(value[None], (count,) + value.shape), axe...  23.6 us
    ppermute x1, starting transfers between devices, body(): half = own + lax.ppermute(other, 'core', [(0, 1), (1, 0)])  22.1 us
    pallas_call x1, Pallas kernels, local_moments(): pl.pallas_call(moments_kernel, grid_spec=pltpu.PrefetchScalarGridSpec(num...  21.9 us
    all_to_all x1, blocking collectives, body(): parts = lax.all_to_all(share.reshape(8, rows, WIDTH), 'z', 0, 0, tiled=True)  15.9 us
    all_to_all x1, waiting for transfers between devices, spread(): lax.all_to_all(jnp.broadcast_to(value[None], (count,) + value.shape), axe...  7.91 us
    pallas_call x1, Pallas kernels, solve_share(): pl.pallas_call(solve_kernel, in_specs=[pl.BlockSpec(memory_space=pltpu.SM...  6.59 us
    ppermute x1, starting transfers between devices, body(): there = lax.ppermute(here, 'core', [(0, 1), (1, 0)])  5.4 us
  transfers between devices with their start and end apart: 3, of which 3 were waited for; matrix products, arithmetic and copies ran while one was open for 0% of the time, Pallas kernels for 0%

profile of v1, /device:TPU:1, one launch (start us, length us, event | category | flops | bytes accessed | tf_op | source)
XLA Modules:
  0.0 152.2 jit_solution(3928609173498503426)
XLA Ops:
  0.6 0.8 copy.21
  1.4 0.8 copy.22.lw_ref
  2.2 0.8 copy.23.mean_ref
  3.0 1.2 copy-done
  4.3 0.7 copy-done.1
  4.9 21.9 %moments.1 = (f32[48,72,128]{2,1,0:T(8,128)S(1)}, f32[48,72,128]{2,1,0:T(8,128)S(1)}) custom-call(s32[19,8]{1,0:T(8,128)S(1)} %bitcast.11, s32[19]{0:T(128)S(1)} %bitcast.12, s32[1]{0:T(128)} %bitcast.3.core, f32[19,5]{1,0:T(8,128)S(1)} %copy.22.lw_ref, bf16[32,128,128]{2,1,0:T(8,128)(2,1)S(1)} %bitcast.10, bf16[19,5,128,128]{3,2,1,0:T(8,128)(2,1)} %fac_ref.1, ...), custom_call_target="tpu_custom_call" | custom-call | tf_op jit(solution)/shard_map/moments/pallas_call | solution.py:171
  26.9 22.1 %collective-permute-start = (f32[48,72,128]{2,1,0:T(8,128)S(1)}, f32[48,72,128]{2,1,0:T(8,128)S(1)}, u32[]{:S(2)}, u32[]{:S(2)}) collective-permute-start(f32[48,72,128]{2,1,0:T(8,128)S(1)} %get-tuple-element.9), channel_id=1, source_target_pairs={{0,1},{1,0},{2,3},{3,2},{4,5},{5,4},{6,7},{7,6},{8,9},{9,8},{10,11... | collective-permute-start | bytes 5308424 | tf_op jit(solution)/shard_map/ppermute | solution.py:323
  48.9 3.3 %collective-permute-done = f32[48,72,128]{2,1,0:T(8,128)S(1)} collective-permute-done((f32[48,72,128]{2,1,0:T(8,128)S(1)}, f32[48,72,128]{2,1,0:T(8,128)S(1)}, u32[]{:S(2)}, u32[]{:S(2)}) %collective-permute-start) | collective-permute-done | bytes 1769504 | tf_op jit(solution)/shard_map/ppermute | solution.py:323
  52.2 0.2 add.26
  52.4 27.1 %all_to_all.20 = f32[48,72,128]{2,1,0:T(8,128)S(1)} all-to-all(f32[48,72,128]{2,1,0:T(8,128)S(1)} %add.26), channel_id=1, replica_groups=mesh['x'=4,'z'=8,'y'=4,'core'=2] {'x','y'}, dimensions={0} | all-to-all | bytes 3538944 | tf_op jit(solution)/shard_map/all_to_all | solution.py:325
  79.6 15.9 %all_to_all.21 = f32[8,27,128]{2,1,0:T(8,128)S(1)} all-to-all(f32[8,27,128]{2,1,0:T(8,128)S(1)} %reshape.46), channel_id=1, replica_groups=mesh['x'=4,'z'=8,'y'=4,'core'=2] {'z'}, dimensions={0} | all-to-all | bytes 221184 | tf_op jit(solution)/shard_map/all_to_all | solution.py:328
  95.5 0.7 broadcast_in_dim.10
  96.2 3.4 %all-to-all-start.2 = ((f32[8,27,128]{2,1,0:T(8,128)}), f32[8,27,128]{2,1,0:T(8,128)S(1)}, u32[]{:S(2)}, u32[]{:S(2)}) async-start(f32[8,27,128]{2,1,0:T(8,128)} %broadcast_in_dim.10), calls=%async_computation.2 | async-start | bytes 262144 | tf_op jit(solution)/shard_map/all_to_all | solution.py:311
  99.6 7.9 %all-to-all-done.2 = f32[8,27,128]{2,1,0:T(8,128)S(1)} async-done(((f32[8,27,128]{2,1,0:T(8,128)}), f32[8,27,128]{2,1,0:T(8,128)S(1)}, u32[]{:S(2)}, u32[]{:S(2)}) %all-to-all-start.2) | async-done | bytes 110624 | tf_op jit(solution)/shard_map/all_to_all | solution.py:311
  107.5 6.6 %solve.1 = f32[3,72,128]{2,1,0:T(8,128)S(1)} custom-call(s32[1]{0:T(128)} %bitcast.first, f32[3,72,128]{2,1,0:T(8,128)S(1)} %reshape.47.share_ref, f32[95,128]{1,0:T(8,128)S(1)} %reshape.48.mean_ref), custom_call_target="tpu_custom_call" | custom-call | tf_op jit(solution)/shard_map/solve/pallas_call | solution.py:262
  114.2 23.6 %all_to_all.22 = f32[16,3,72,128]{3,2,1,0:T(8,128)S(1)} all-to-all(f32[16,3,72,128]{3,2,1,0:T(8,128)S(1)} %broadcast_in_dim.22), channel_id=1, replica_groups=mesh['x'=4,'z'=8,'y'=4,'core'=2] {'x','y'}, dimensions={0} | all-to-all | bytes 3538944 | tf_op jit(solution)/shard_map/all_to_all | solution.py:311
  137.8 5.4 %collective-permute-start.1 = (f32[48,72,128]{2,1,0:T(8,128)S(1)}, f32[48,72,128]{2,1,0:T(8,128)S(1)}, u32[]{:S(2)}, u32[]{:S(2)}) collective-permute-start(f32[48,72,128]{2,1,0:T(8,128)S(1)} %bitcast.13), channel_id=1, source_target_pairs={{0,1},{1,0},{2,3},{3,2},{4,5},{5,4},{6,7},{7,6},{8,9},{9,8},{10,11... | collective-permute-start | bytes 5308424 | tf_op jit(solution)/shard_map/ppermute | solution.py:334
  143.2 3.3 %collective-permute-done.1 = f32[48,72,128]{2,1,0:T(8,128)S(1)} collective-permute-done((f32[48,72,128]{2,1,0:T(8,128)S(1)}, f32[48,72,128]{2,1,0:T(8,128)S(1)}, u32[]{:S(2)}, u32[]{:S(2)}) %collective-permute-start.1) | collective-permute-done | bytes 1769504 | tf_op jit(solution)/shard_map/ppermute | solution.py:334
  146.5 0.2 maximum_select_fusion.packed_ref
  146.8 3.8 %unpack.1 = (f32[95,128,128]{2,1,0:T(8,128)}, f32[5,19,128]{2,1,0:T(8,128)S(1)}, f32[5,19,128]{2,1,0:T(8,128)S(1)}) custom-call(f32[96,72,128]{2,1,0:T(8,128)S(1)} %maximum_select_fusion.packed_ref), custom_call_target="tpu_custom_call" | custom-call | tf_op jit(solution)/shard_map/unpack/pallas_call | solution.py:291
  150.6 0.2 slice_reduce_fusion
  150.9 0.1 copy.30
  151.0 0.6 copy.26
  151.6 0.6 bitcast_subtract_fusion
  (11 shorter events, 0.3 us)
Async XLA Ops:
  3.0 1.2 copy-start
  4.3 0.7 copy-start.1
  26.9 25.4 %collective-permute-start = (f32[48,72,128]{2,1,0:T(8,128)S(1)}, f32[48,72,128]{2,1,0:T(8,128)S(1)}, u32[]{:S(2)}, u32[]{:S(2)}) collective-permute-start(f32[48,72,128]{2,1,0:T(8,128)S(1)} %get-tuple-element.9), channel_id=1, source_target_pairs={{0,1},{1,0},{2,3},{3,2},{4,5},{5,4},{6,7},{7,6},{8,9},{9,8},{10,11... | collective-permute-start | bytes 5308424 | tf_op jit(solution)/shard_map/ppermute | solution.py:323
  96.2 11.3 %all-to-all-start.2 = ((f32[8,27,128]{2,1,0:T(8,128)}), f32[8,27,128]{2,1,0:T(8,128)S(1)}, u32[]{:S(2)}, u32[]{:S(2)}) async-start(f32[8,27,128]{2,1,0:T(8,128)} %broadcast_in_dim.10), calls=%async_computation.2 | async-start | bytes 262144 | tf_op jit(solution)/shard_map/all_to_all | solution.py:311
  137.8 8.7 %collective-permute-start.1 = (f32[48,72,128]{2,1,0:T(8,128)S(1)}, f32[48,72,128]{2,1,0:T(8,128)S(1)}, u32[]{:S(2)}, u32[]{:S(2)}) collective-permute-start(f32[48,72,128]{2,1,0:T(8,128)S(1)} %bitcast.13), channel_id=1, source_target_pairs={{0,1},{1,0},{2,3},{3,2},{4,5},{5,4},{6,7},{7,6},{8,9},{9,8},{10,11... | collective-permute-start | bytes 5308424 | tf_op jit(solution)/shard_map/ppermute | solution.py:334

commit v2 on v1

v2 whole, which is shorter than its diff:
```python
import functools
import jax
import jax.numpy as jnp
from jax import lax
from jax.experimental import pallas as pl
from jax.experimental.pallas import tpu as pltpu
from jax.sharding import Mesh, PartitionSpec as P

CLASSES = 19
COMPS = 5
WIDTH = 128
BLOCK = 128
ROWS = 72
STRIPS = 16
F32 = jnp.float32
BF16 = jnp.bfloat16
SLOTS = 9
GROUP = 3
OWNERS = 16
HALF = GROUP * OWNERS
SHARE = 224
PART = SHARE // 2
VMEM_LIMIT = 48 * 1024 * 1024


def iota(shape, axis):
    return lax.broadcasted_iota(jnp.int32, shape, axis)


def pieces(value, count):
    out = []
    for _ in range(count):
        part = value.astype(BF16)
        out.append(part)
        value = value - part.astype(F32)
    return out


def pack_strips(strips, extra):
    lane = iota((8, WIDTH), 1)
    out = [strips[0]]
    for s in range(1, 8):
        moved = pltpu.roll(strips[16 - s], 8 * s, 1)
        out.append(jnp.where(lane >= 8 * s, strips[s], moved))
    out.append(jnp.where(lane >= 64, strips[8], extra))
    return out


def unpack_strips(slots):
    lane = iota((8, WIDTH), 1)
    strips = [None] * 16
    strips[0] = slots[0]
    for s in range(1, 8):
        strips[s] = jnp.where(lane >= 8 * s, slots[s], 0.0)
        moved = pltpu.roll(slots[s], WIDTH - 8 * s, 1)
        strips[16 - s] = jnp.where(lane >= WIDTH - 8 * s, moved, 0.0)
    strips[8] = jnp.where(lane >= 64, slots[8], 0.0)
    return strips


def extra_rows(row, count):
    sub = iota((8, WIDTH), 0)
    later = pltpu.roll(jnp.broadcast_to(row, (8, WIDTH)), 64, 1)
    return jnp.where(sub == 0, row, jnp.where(sub == 1, later, jnp.where(sub == 2, count, 0.0)))


def split_extra(slot):
    lane = iota((8, WIDTH), 1)
    moved = pltpu.roll(slot, 64, 1)
    row = jnp.where(lane[0:1] < 64, slot[0:1], moved[1:2])
    count = jnp.where(lane[0:1] < 64, slot[2:3], moved[2:3])
    return row, count


def moments_kernel(lists, list_counts, core, lw_ref, emb_ref, fac_ref, mean_ref, own_ref, other_ref,
                   acc, tot, cnt, flipped, shift, const, rows_t, gate, items):
    sub = iota((8, WIDTH), 0)
    lane = iota((8, WIDTH), 1)
    ident = (iota((WIDTH, WIDTH), 0) == iota((WIDTH, WIDTH), 1)).astype(F32).astype(BF16)

    acc[...] = jnp.zeros_like(acc)
    tot[...] = jnp.zeros_like(tot)
    cnt[...] = jnp.zeros_like(cnt)
    gate[...] = jnp.zeros_like(gate)
    rows_t[...] = jnp.zeros_like(rows_t)

    def list_class(c, at):
        n = list_counts[c]

        def list_pair(t, at):
            items[0, at] = c
            items[1, at] = lists[2 * t, c]
            items[2, at] = lists[2 * t + 1, c]
            items[3, at] = jnp.where(2 * t + 1 < n, 2 * BLOCK, BLOCK)
            return at + 1

        return lax.fori_loop(0, (n + 1) // 2, list_pair, at)

    total_items = lax.fori_loop(0, CLASSES, list_class, jnp.int32(0))

    def half_step(i, now, before):
        at_sum = jnp.minimum(jnp.maximum(i - 2, 0), total_items - 1)
        at_score = jnp.minimum(jnp.maximum(i - 1, 0), total_items - 1)
        at_class = jnp.minimum(i, total_items - 1)

        c = items[0, at_sum]
        rows = jnp.concatenate([emb_ref[items[1, at_sum]], emb_ref[items[2, at_sum]]], axis=0)
        weights = gate[before]
        flat = rows_t[before]
        both = jnp.concatenate([rows, rows], axis=0)
        scaled = []
        for k in range(COMPS):
            high, low = pieces(flat * weights[k : k + 1], 2)
            scaled.append(jnp.concatenate([high, low], axis=1))
        for k in range(COMPS):
            acc[c * COMPS + k] += jnp.dot(scaled[k], both, preferred_element_type=F32)
        tall = jnp.concatenate([weights, jnp.zeros_like(weights)])
        sums = jnp.dot(jnp.concatenate(pieces(tall, 3)), rows, preferred_element_type=F32)
        tot[c] += sums[0:8] + sums[16:24] + sums[32:40]
        cnt[c] += weights[:, :BLOCK] + weights[:, BLOCK:]

        first = emb_ref[items[1, at_score]].astype(F32).T
        later = emb_ref[items[2, at_score]].astype(F32).T
        flat = jnp.concatenate([first, later], axis=1)
        square = jnp.zeros((8, 2 * BLOCK), F32)
        wide_sub = iota((8, 2 * BLOCK), 0)
        flat_half = flat.astype(BF16)
        for k in range(COMPS):
            offset = shift[before, k]
            centred = jnp.dot(flipped[before, k], flat_half, preferred_element_type=F32)
            centred = centred - jnp.concatenate([offset, offset], axis=1)
            line = jnp.sum(centred * centred, axis=0, keepdims=True)
            square = jnp.where(wide_sub == k, line, square)
        consts = const[before]
        scores = jnp.concatenate([consts, consts], axis=1) - 0.5 * square
        top = jnp.max(scores, axis=0, keepdims=True)
        weights = jnp.exp(scores - top)
        weights = weights / jnp.sum(weights, axis=0, keepdims=True)
        live = jnp.where((i >= 1) & (i <= total_items), items[3, at_score], 0)
        gate[now] = jnp.where(iota((8, 2 * BLOCK), 1) < live, weights, 0.0)
        rows_t[now] = flat

        c = items[0, at_class]
        diag = jnp.ones((8, WIDTH), F32)
        prior = jnp.full((8, WIDTH), -1e30, F32)
        mean = mean_ref[:, c]
        mean_pieces = jnp.concatenate(
            pieces(jnp.concatenate([mean, jnp.zeros((16 - COMPS, WIDTH), F32)]), 3)
        )
        for k in range(COMPS):
            factor = fac_ref[c, k]
            wide = factor.astype(F32)
            on_diag = None
            for s in range(STRIPS):
                part = jnp.where(lane - 8 * s == sub, wide[8 * s : 8 * s + 8], 0.0)
                on_diag = part if on_diag is None else on_diag + part
            diag = jnp.where(sub == k, jnp.sum(on_diag, axis=0, keepdims=True), diag)
            prior = jnp.where(sub == k, lw_ref[k, c], prior)
            flipped[now, k] = wide.T.astype(BF16)
            parts = jnp.dot(mean_pieces, factor, preferred_element_type=F32)
            line = parts[k : k + 1] + parts[16 + k : 17 + k] + parts[32 + k : 33 + k]
            shift[now, k] = jnp.broadcast_to(line, (WIDTH, WIDTH)).T
        const[now] = jnp.sum(jnp.log(diag), axis=1, keepdims=True) + prior

    def step(i, carry):
        half_step(2 * i, 0, 1)
        half_step(2 * i + 1, 1, 0)
        return carry

    lax.fori_loop(0, (total_items + 3) // 2, step, 0)

    def pack(q, carry):
        for base, out_ref in ((core[0], own_ref), (1 - core[0], other_ref)):
            for r in range(GROUP):
                slot = base * HALF + q * GROUP + r
                c = slot // COMPS
                k = slot - c * COMPS
                counted = cnt[c, pl.ds(k, 1), :]
                count = jnp.broadcast_to(jnp.sum(counted, axis=1, keepdims=True), (1, WIDTH))
                slots = pack_strips(
                    [acc[slot, 8 * s : 8 * s + 8, :] for s in range(STRIPS)],
                    extra_rows(tot[c, pl.ds(k, 1), :], count),
                )
                for s in range(SLOTS):
                    out_ref[q, r * ROWS + 8 * s : r * ROWS + 8 * s + 8, :] = slots[s]
            out_ref[q, GROUP * ROWS : SHARE, :] = jnp.zeros((SHARE - GROUP * ROWS, WIDTH), F32)
        return carry

    lax.fori_loop(0, OWNERS, pack, 0)


def local_moments(blocks, lists, list_counts, core, log_weights, factors, means):
    vmem = pl.BlockSpec(memory_space=pltpu.VMEM)
    smem = pl.BlockSpec(memory_space=pltpu.SMEM)
    return pl.pallas_call(
        moments_kernel,
        in_specs=[smem, smem, smem, smem, vmem, vmem, vmem],
        out_specs=[vmem, vmem],
        scratch_shapes=[
            pltpu.VMEM(((CLASSES + 1) * COMPS, WIDTH, WIDTH), F32),
            pltpu.VMEM((CLASSES + 1, 8, WIDTH), F32),
            pltpu.VMEM((CLASSES + 1, 8, WIDTH), F32),
            pltpu.VMEM((2, COMPS, WIDTH, WIDTH), BF16),
            pltpu.VMEM((2, COMPS, WIDTH, WIDTH), F32),
            pltpu.VMEM((2, 8, WIDTH), F32),
            pltpu.VMEM((2, WIDTH, 2 * BLOCK), F32),
            pltpu.VMEM((2, 8, 2 * BLOCK), F32),
            pltpu.SMEM((4, 128), jnp.int32),
        ],
        out_shape=[jax.ShapeDtypeStruct((OWNERS, SHARE, WIDTH), F32)] * 2,
        compiler_params=pltpu.CompilerParams(vmem_limit_bytes=VMEM_LIMIT),
        name="moments",
    )(lists, list_counts, core, log_weights, blocks, factors, means)


def solve_kernel(place, mine_ref, theirs_ref, mean_ref, out_ref):
    lane = iota((8, WIDTH), 1)
    sub = iota((8, WIDTH), 0)
    early = place[1] == 0
    share = []
    for at in range(2):
        for t in range(PART // 8):
            cut = slice(8 * t, 8 * t + 8)
            share.append(jnp.where(early == (at == 0), mine_ref[cut, :], theirs_ref[cut, :]))
    strips, new_means, counts = [], [], []
    for g in range(GROUP):
        slots = share[SLOTS * g : SLOTS * g + SLOTS]
        totals, count = split_extra(slots[8])
        comp = jnp.minimum(place[0] + g, CLASSES * COMPS - 1)
        old = mean_ref[lax.rem(comp, COMPS), pl.ds(comp // COMPS, 1), :]
        denom = count + 1.0
        new = (totals + old) / denom
        old_t = jnp.broadcast_to(old, (WIDTH, WIDTH)).T
        new_t = jnp.broadcast_to(new * denom, (WIDTH, WIDTH)).T
        second = unpack_strips(slots)
        rows = []
        for s in range(STRIPS):
            cut = slice(8 * s, 8 * s + 8)
            scatter = second[s] + old_t[cut] * old - new_t[cut] * new
            scatter = jnp.where(lane - 8 * s == sub, scatter + 1.0, scatter)
            rows.append(jnp.where(lane >= 8 * s, scatter / denom, 0.0))
        strips.append(rows)
        new_means.append(new)
        counts.append(count)
    for s in range(STRIPS):
        for g in range(GROUP):
            rows = strips[g]
            panel = rows[s]
            columns = [
                jnp.broadcast_to(panel[:, 8 * s + j : 8 * s + j + 1], (8, WIDTH)) for j in range(8)
            ]
            block = (lane >= 8 * s) & (lane < 8 * s + 8)
            panel = jnp.where(block, jnp.where(lane - 8 * s == sub, 1.0, 0.0), panel)
            pivots = jnp.ones((8, WIDTH), F32)
            for j in range(8):
                pivot = columns[j][j : j + 1]
                pivots = jnp.where(sub == j, pivot, pivots)
                if j < 7:
                    ratio = jnp.where(sub > j, columns[j] * (1.0 / pivot), 0.0)
                    panel = panel - ratio * panel[j : j + 1]
                    for l in range(j + 1, 8):
                        columns[l] = columns[l] - ratio * columns[l][j : j + 1]
            panel = panel * (1.0 / jnp.sqrt(pivots))
            rows[s] = panel
            if s < STRIPS - 1:
                a, b, d = [p.astype(F32) for p in pieces(panel, 3)]
                left = jnp.concatenate([a, a, b, b, a, d], axis=0).astype(BF16)
                right = jnp.concatenate([a, b, a, b, d, a], axis=0).astype(BF16)
                change = lax.dot_general(
                    left, right, (((0,), (0,)), ((), ())), preferred_element_type=F32
                )
                for t in range(s + 1, STRIPS):
                    base = jnp.where(block, 0.0, rows[t])
                    rows[t] = base - change[8 * t : 8 * t + 8]
    packed = []
    for g in range(GROUP):
        lower = jnp.concatenate(
            [jnp.where(lane - 8 * s <= sub, strips[g][s], 0.0) for s in range(STRIPS)], axis=0
        )
        upper = lower.T
        packed += pack_strips(
            [upper[8 * s : 8 * s + 8] for s in range(STRIPS)],
            extra_rows(new_means[g], counts[g]),
        )
    packed.append(jnp.zeros((8, WIDTH), F32))
    for t in range(PART // 8):
        out_ref[8 * t : 8 * t + 8, :] = jnp.where(early, packed[t], packed[PART // 8 + t])


def solve_share(place, mine, theirs, means):
    smem = pl.BlockSpec(memory_space=pltpu.SMEM)
    vmem = pl.BlockSpec(memory_space=pltpu.VMEM)
    return pl.pallas_call(
        solve_kernel,
        in_specs=[smem, vmem, vmem, vmem],
        out_specs=vmem,
        out_shape=jax.ShapeDtypeStruct((PART, WIDTH), F32),
        compiler_params=pltpu.CompilerParams(vmem_limit_bytes=VMEM_LIMIT),
        name="solve",
    )(place, mine, theirs, means)


UNPACK = 19


def unpack_kernel(core, here_ref, there_ref, factor_ref, mean_ref, log_ref, counts):
    step = pl.program_id(0)
    for g in range(UNPACK):
        comp = step * UNPACK + g
        half = jnp.where(comp >= HALF, 1, 0)
        at = comp - half * HALF
        q = at // GROUP
        first = pl.multiple_of((at - q * GROUP) * ROWS, 8)
        here = half == core[0]
        slots = []
        for s in range(SLOTS):
            cut = pl.ds(first + 8 * s, 8)
            slots.append(jnp.where(here, here_ref[q, cut, :], there_ref[q, cut, :]))
        strips = unpack_strips(slots)
        for s in range(STRIPS):
            factor_ref[g, 8 * s : 8 * s + 8, :] = strips[s]
        row, count = split_extra(slots[8])
        c = comp // COMPS
        k = comp - c * COMPS
        mean_ref[k, pl.ds(c, 1), :] = row
        counts[k, pl.ds(c, 1), :] = count

    @pl.when(step == CLASSES * COMPS // UNPACK - 1)
    def _():
        mask = iota((CLASSES, WIDTH), 0) == iota((CLASSES, WIDTH), 1)
        values = [counts[k] for k in range(COMPS)]
        total = jnp.log(sum(values) + float(COMPS))
        for k in range(COMPS):
            logs = jnp.where(mask, jnp.log(values[k] + 1.0) - total, 0.0)
            log_ref[k : k + 1, :] = jnp.sum(logs, axis=0, keepdims=True)[:, :CLASSES]


def unpack_all(core, here, there):
    steps = CLASSES * COMPS // UNPACK
    vmem = pl.BlockSpec(memory_space=pltpu.VMEM)
    return pl.pallas_call(
        unpack_kernel,
        grid=(steps,),
        in_specs=[pl.BlockSpec(memory_space=pltpu.SMEM), vmem, vmem],
        out_specs=[
            pl.BlockSpec((UNPACK, WIDTH, WIDTH), lambda i: (i, 0, 0)),
            pl.BlockSpec((COMPS, CLASSES, WIDTH), lambda i: (0, 0, 0)),
            pl.BlockSpec((COMPS, CLASSES), lambda i: (0, 0)),
        ],
        out_shape=[
            jax.ShapeDtypeStruct((CLASSES * COMPS, WIDTH, WIDTH), F32),
            jax.ShapeDtypeStruct((COMPS, CLASSES, WIDTH), F32),
            jax.ShapeDtypeStruct((COMPS, CLASSES), F32),
        ],
        scratch_shapes=[pltpu.VMEM((COMPS, CLASSES, WIDTH), F32)],
        compiler_params=pltpu.CompilerParams(vmem_limit_bytes=VMEM_LIMIT),
        name="unpack",
    )(core, here, there)


def swap_cores(value):
    return lax.ppermute(value, "core", [(0, 1), (1, 0)])


def sum_far(value):
    total = value
    for hop in (2, 1, 3):
        total = total + lax.ppermute(value, "far", [(i, (i + hop) % 4) for i in range(4)])
    return total


def body(embeddings, class_blocks, class_counts, means, log_weights, factors):
    frames_here, pixels_here, width = embeddings.shape
    blocks = embeddings.reshape(frames_here * pixels_here // BLOCK, BLOCK, width)
    core = lax.axis_index("core").astype(jnp.int32)
    near = lax.axis_index("near").astype(jnp.int32)
    owner = (lax.axis_index("x") * 4 + lax.axis_index("y")).astype(jnp.int32)
    means_t = jnp.transpose(means, (1, 0, 2))
    own, other = local_moments(
        blocks, class_blocks[0, 0].T, class_counts[0, 0], core[None], log_weights.T, factors, means_t
    )
    peers = ("x", "y", "near")
    half = own + swap_cores(other)
    parts = lax.all_to_all(half.reshape(2 * OWNERS, PART, width), peers, 0, 0, tiled=True)
    mine = sum_far(jnp.sum(parts, axis=0))
    theirs = lax.ppermute(mine, "near", [(0, 1), (1, 0)])
    place = jnp.stack([core * HALF + owner * GROUP, near])
    solved = solve_share(place, mine, theirs, means_t)
    spread = jnp.broadcast_to(solved[None], (2 * OWNERS, PART, width))
    here = lax.all_to_all(spread, peers, 0, 0, tiled=True).reshape(OWNERS, SHARE, width)
    there = swap_cores(here)
    new_factor, new_mean, new_log = unpack_all(core[None], here, there)
    return (
        new_log.T,
        jnp.transpose(new_mean, (1, 0, 2)),
        new_factor.reshape(CLASSES, COMPS, width, width),
    )


def solution(mesh):
    wide = Mesh(mesh.devices.reshape(4, 4, 2, 4, 2), ("x", "far", "near", "y", "core"))
    space = ("far", "near", "y", "core")
    return jax.shard_map(
        body,
        mesh=wide,
        in_specs=(P("x", space, None), P("x", space, None, None), P("x", space, None), P(), P(), P()),
        out_specs=(P(), P(), P()),
        check_vma=False,
    )
```

time: 154 us -> 124 us (0.81); the launches traced: 152 us -> 124 us
  starting transfers between devices: 30.8 us -> 18 us
  blocking collectives: 66.5 us -> 56.5 us
  Pallas kernels: 32.4 us -> 29 us
  local copies, waits for them, and re-layouts: 5.85 us -> 4.2 us
    all_to_all x3 -> x2, blocking collectives: 66.5 us -> 56.5 us  [the longest x1 31.6 us: body(): lax.all_to_all(half.reshape(2 * OWNERS, PART, width), peers, 0, 0, tiled=...]
    ppermute x2 -> x6, starting transfers between devices: 27.5 us -> 18 us  [the longest x2 10.1 us: swap_cores(): return lax.ppermute(value, 'core', [(0, 1), (1, 0)])]
    ppermute x2 -> x6, waiting for transfers between devices: 6.64 us -> 15.2 us  [the longest x2 6.82 us: swap_cores(): return lax.ppermute(value, 'core', [(0, 1), (1, 0)])]
    all_to_all x1 -> x0, waiting for transfers between devices: 7.91 us -> none  [spread(): lax.all_to_all(jnp.broadcast_to(value[None], (count,) + value.shape), axe...]
    all_to_all x1 -> x0, starting transfers between devices: 3.37 us -> none  [spread(): lax.all_to_all(jnp.broadcast_to(value[None], (count,) + value.shape), axe...]
    pallas_call x3, Pallas kernels: 32.4 us -> 29 us  [the longest x1 17.6 us: local_moments(): pl.pallas_call(moments_kernel, in_specs=[smem, smem, smem, smem, vmem, vm...]
    unnamed x9 -> x12, local copies, waits for them, and re-layouts: 5.02 us -> 4.08 us
  transfers between devices with their start and end apart: 3 -> 6, of which waited for: 3 -> 5; matrix products, arithmetic and copies ran while one was open for 0% -> 0% of each run, Pallas kernels for 0% -> 0%
where the time goes in v2:
time: 124 us
  blocking collectives  56.5 us (46%)
  Pallas kernels  29 us (23%)
  starting transfers between devices  18 us (15%)
  waiting for transfers between devices  15.2 us (12%)
  local copies, waits for them, and re-layouts  4.2 us (3%)
    all_to_all x1, blocking collectives, body(): lax.all_to_all(half.reshape(2 * OWNERS, PART, width), peers, 0, 0, tiled=...  31.6 us
    all_to_all x1, blocking collectives, body(): lax.all_to_all(spread, peers, 0, 0, tiled=True)  24.9 us
    pallas_call x1, Pallas kernels, local_moments(): pl.pallas_call(moments_kernel, in_specs=[smem, smem, smem, smem, vmem, vm...  17.6 us
    ppermute x2, starting transfers between devices, swap_cores(): return lax.ppermute(value, 'core', [(0, 1), (1, 0)])  10.1 us
    ppermute x3, starting transfers between devices, sum_far(): lax.ppermute(value, 'far', [(i, (i + hop) % 4) for i in range(4)])  7.69 us
    pallas_call x1, Pallas kernels, solve_share(): pl.pallas_call(solve_kernel, in_specs=[smem, vmem, vmem, vmem], out_specs...  7.14 us
    ppermute x2, waiting for transfers between devices, swap_cores(): return lax.ppermute(value, 'core', [(0, 1), (1, 0)])  6.82 us
    ppermute x3, waiting for transfers between devices, sum_far(): lax.ppermute(value, 'far', [(i, (i + hop) % 4) for i in range(4)])  4.97 us
  transfers between devices with their start and end apart: 6, of which 5 were waited for; matrix products, arithmetic and copies ran while one was open for 0% of the time, Pallas kernels for 0%

profile of v2, /device:TPU:1, one launch (start us, length us, event | category | flops | bytes accessed | tf_op | source)
XLA Modules:
  0.0 124.1 jit_solution(18086901143699898812)
XLA Ops:
  0.6 1.2 copy-done
  1.9 0.8 copy-done.1
  2.7 0.7 copy-done.3
  3.4 0.7 copy-done.4
  4.1 0.7 copy-done.5
  4.7 17.6 %moments.1 = (f32[16,224,128]{2,1,0:T(8,128)S(1)}, f32[16,224,128]{2,1,0:T(8,128)S(1)}) custom-call(s32[8,19]{1,0:T(8,128)S(1)} %bitcast.20, s32[19]{0:T(128)S(1)} %bitcast.22, s32[1]{0:T(128)} %bitcast.core, f32[5,19]{1,0:T(8,128)S(1)} %bitcast.21, bf16[32,128,128]{2,1,0:T(8,128)(2,1)S(1)} %bitcast.17, bf16[19,5,128,128]{3,2,1,0:T(8,128)(2,1)} %fac_ref.1, ...), custom_call_target="tpu_custom_call" | custom-call | tf_op jit(solution)/shard_map/moments/pallas_call | solution.py:195
  22.3 4.4 %collective-permute-start = (f32[16,224,128]{2,1,0:T(8,128)S(1)}, f32[16,224,128]{2,1,0:T(8,128)S(1)}, u32[]{:S(2)}, u32[]{:S(2)}) collective-permute-start(f32[16,224,128]{2,1,0:T(8,128)S(1)} %get-tuple-element.9), channel_id=1, source_target_pairs={{0,1},{1,0},{2,3},{3,2},{4,5},{5,4},{6,7},{7,6},{8,9},{9,8},{10,11... | collective-permute-start | bytes 5505032 | tf_op jit(solution)/shard_map/ppermute | solution.py:362
  26.7 3.4 %collective-permute-done = f32[16,224,128]{2,1,0:T(8,128)S(1)} collective-permute-done((f32[16,224,128]{2,1,0:T(8,128)S(1)}, f32[16,224,128]{2,1,0:T(8,128)S(1)}, u32[]{:S(2)}, u32[]{:S(2)}) %collective-permute-start) | collective-permute-done | bytes 1835040 | tf_op jit(solution)/shard_map/ppermute | solution.py:362
  30.1 0.3 add.20
  30.4 31.6 %all_to_all.10 = f32[32,112,128]{2,1,0:T(8,128)S(1)} all-to-all(f32[32,112,128]{2,1,0:T(8,128)S(1)} %bitcast.23), channel_id=1, replica_groups=mesh['x'=4,'far'=4,'near'=2,'y'=4,'core'=2] {'x','y','near'}, dimensions={0} | all-to-all | bytes 3670016 | tf_op jit(solution)/shard_map/all_to_all | solution.py:384
  62.0 0.1 reduce_sum.9
  62.1 5.5 %collective-permute-start.3 = (f32[112,128]{1,0:T(8,128)S(1)}, f32[112,128]{1,0:T(8,128)S(1)}, u32[]{:S(2)}, u32[]{:S(2)}) collective-permute-start(f32[112,128]{1,0:T(8,128)S(1)} %reduce_sum.9), channel_id=1, source_target_pairs={{0,48},{16,0},{32,16},{48,32},{1,49},{17,1},{33,17},{49,33},{2,50}... | collective-permute-start | bytes 172040 | tf_op jit(solution)/shard_map/ppermute | solution.py:368
  67.7 2.2 %collective-permute-start.1 = (f32[112,128]{1,0:T(8,128)S(1)}, f32[112,128]{1,0:T(8,128)S(1)}, u32[]{:S(2)}, u32[]{:S(2)}) collective-permute-start(f32[112,128]{1,0:T(8,128)S(1)} %reduce_sum.9), channel_id=1, source_target_pairs={{0,32},{16,48},{32,0},{48,16},{1,33},{17,49},{33,1},{49,17},{2,34}... | collective-permute-start | bytes 172040 | tf_op jit(solution)/shard_map/ppermute | solution.py:368
  69.8 3.6 %collective-permute-done.2 = f32[112,128]{1,0:T(8,128)S(1)} collective-permute-done((f32[112,128]{1,0:T(8,128)S(1)}, f32[112,128]{1,0:T(8,128)S(1)}, u32[]{:S(2)}, u32[]{:S(2)}) %collective-permute-start.2) | collective-permute-done | bytes 57376 | tf_op jit(solution)/shard_map/ppermute | solution.py:368
  73.4 1.4 %collective-permute-done.1 = f32[112,128]{1,0:T(8,128)S(1)} collective-permute-done((f32[112,128]{1,0:T(8,128)S(1)}, f32[112,128]{1,0:T(8,128)S(1)}, u32[]{:S(2)}, u32[]{:S(2)}) %collective-permute-start.1) | collective-permute-done | bytes 57376 | tf_op jit(solution)/shard_map/ppermute | solution.py:368
  74.8 0.2 collective-permute-start.4
  75.0 0.1 pad_add_fusion.place
  75.1 3.4 %collective-permute-done.4.theirs_ref = f32[112,128]{1,0:T(8,128)S(1)} collective-permute-done((f32[112,128]{1,0:T(8,128)S(1)}, f32[112,128]{1,0:T(8,128)S(1)}, u32[]{:S(2)}, u32[]{:S(2)}) %collective-permute-start.4) | collective-permute-done | bytes 57376 | tf_op jit(solution)/shard_map/ppermute | solution.py:386
  78.5 7.1 %solve.1 = f32[112,128]{1,0:T(8,128)S(1)} custom-call(s32[2]{0:T(128)S(1)} %pad_add_fusion.place, f32[112,128]{1,0:T(8,128)S(1)} %add_add_fusion.mine_ref, f32[112,128]{1,0:T(8,128)S(1)} %collective-permute-done.4.theirs_ref, f32[5,19,128]{2,1,0:T(8,128)S(1)} %bitcast.19), custom_call_target="tpu_custom_call" | custom-call | tf_op jit(solution)/shard_map/solve/pallas_call | solution.py:293
  85.7 0.1 broadcast_in_dim.5
  85.8 24.9 %all_to_all.11 = f32[32,112,128]{2,1,0:T(8,128)S(1)} all-to-all(f32[32,112,128]{2,1,0:T(8,128)S(1)} %broadcast_in_dim.5), channel_id=1, replica_groups=mesh['x'=4,'far'=4,'near'=2,'y'=4,'core'=2] {'x','y','near'}, dimensions={0} | all-to-all | bytes 3670016 | tf_op jit(solution)/shard_map/all_to_all | solution.py:390
  110.7 5.7 %collective-permute-start.5 = (f32[16,224,128]{2,1,0:T(8,128)S(1)}, f32[16,224,128]{2,1,0:T(8,128)S(1)}, u32[]{:S(2)}, u32[]{:S(2)}) collective-permute-start(f32[16,224,128]{2,1,0:T(8,128)S(1)} %bitcast.15), channel_id=1, source_target_pairs={{0,1},{1,0},{2,3},{3,2},{4,5},{5,4},{6,7},{7,6},{8,9},{9,8},{10,11... | collective-permute-start | bytes 5505032 | tf_op jit(solution)/shard_map/ppermute | solution.py:362
  116.4 3.4 %collective-permute-done.5.there_ref = f32[16,224,128]{2,1,0:T(8,128)S(1)} collective-permute-done((f32[16,224,128]{2,1,0:T(8,128)S(1)}, f32[16,224,128]{2,1,0:T(8,128)S(1)}, u32[]{:S(2)}, u32[]{:S(2)}) %collective-permute-start.5) | collective-permute-done | bytes 1835040 | tf_op jit(solution)/shard_map/ppermute | solution.py:362
  119.8 4.3 %unpack.1 = (f32[95,128,128]{2,1,0:T(8,128)}, f32[5,19,128]{2,1,0:T(8,128)}, f32[5,19]{1,0:T(8,128)}) custom-call(s32[1]{0:T(128)} %bitcast.core, f32[16,224,128]{2,1,0:T(8,128)S(1)} %bitcast.16, f32[16,224,128]{2,1,0:T(8,128)S(1)} %collective-permute-done.5.there_ref), custom_call_target="tpu_custom_call" | custom-call | tf_op jit(solution)/shard_map/unpack/pallas_call | solution.py:341
  (10 shorter events, 0.0 us)
Async XLA Ops:
  0.6 1.2 copy-start
  1.9 0.8 copy-start.1
  2.7 0.7 copy-start.3
  3.4 0.7 copy-start.4
  4.1 0.7 copy-start.5
  22.3 7.8 %collective-permute-start = (f32[16,224,128]{2,1,0:T(8,128)S(1)}, f32[16,224,128]{2,1,0:T(8,128)S(1)}, u32[]{:S(2)}, u32[]{:S(2)}) collective-permute-start(f32[16,224,128]{2,1,0:T(8,128)S(1)} %get-tuple-element.9), channel_id=1, source_target_pairs={{0,1},{1,0},{2,3},{3,2},{4,5},{5,4},{6,7},{7,6},{8,9},{9,8},{10,11... | collective-permute-start | bytes 5505032 | tf_op jit(solution)/shard_map/ppermute | solution.py:362
  62.0 16.5 %copy-start.2 = (f32[19,5,128]{2,0,1:T(8,128)S(1)}, f32[19,5,128]{2,0,1:T(8,128)}, u32[]{:S(2)}) copy-start(f32[19,5,128]{2,0,1:T(8,128)} %param.9) | copy-start | bytes 145924
  62.1 7.7 %collective-permute-start.3 = (f32[112,128]{1,0:T(8,128)S(1)}, f32[112,128]{1,0:T(8,128)S(1)}, u32[]{:S(2)}, u32[]{:S(2)}) collective-permute-start(f32[112,128]{1,0:T(8,128)S(1)} %reduce_sum.9), channel_id=1, source_target_pairs={{0,48},{16,0},{32,16},{48,32},{1,49},{17,1},{33,17},{49,33},{2,50}... | collective-permute-start | bytes 172040 | tf_op jit(solution)/shard_map/ppermute | solution.py:368
  67.6 5.8 %collective-permute-start.2 = (f32[112,128]{1,0:T(8,128)S(1)}, f32[112,128]{1,0:T(8,128)S(1)}, u32[]{:S(2)}, u32[]{:S(2)}) collective-permute-start(f32[112,128]{1,0:T(8,128)S(1)} %reduce_sum.9), channel_id=1, source_target_pairs={{0,16},{16,32},{32,48},{48,0},{1,17},{17,33},{33,49},{49,1},{2,18}... | collective-permute-start | bytes 172040 | tf_op jit(solution)/shard_map/ppermute | solution.py:368
  67.7 7.1 %collective-permute-start.1 = (f32[112,128]{1,0:T(8,128)S(1)}, f32[112,128]{1,0:T(8,128)S(1)}, u32[]{:S(2)}, u32[]{:S(2)}) collective-permute-start(f32[112,128]{1,0:T(8,128)S(1)} %reduce_sum.9), channel_id=1, source_target_pairs={{0,32},{16,48},{32,0},{48,16},{1,33},{17,49},{33,1},{49,17},{2,34}... | collective-permute-start | bytes 172040 | tf_op jit(solution)/shard_map/ppermute | solution.py:368
  74.8 3.7 %collective-permute-start.4 = (f32[112,128]{1,0:T(8,128)S(1)}, f32[112,128]{1,0:T(8,128)S(1)}, u32[]{:S(2)}, u32[]{:S(2)}) collective-permute-start(f32[112,128]{1,0:T(8,128)S(1)} %add_add_fusion.mine_ref), channel_id=1, source_target_pairs={{0,8},{8,0},{1,9},{9,1},{2,10},{10,2},{3,11},{11,3},{4,12},{12,4},... | collective-permute-start | bytes 172040 | tf_op jit(solution)/shard_map/ppermute | solution.py:386
  110.7 9.2 %collective-permute-start.5 = (f32[16,224,128]{2,1,0:T(8,128)S(1)}, f32[16,224,128]{2,1,0:T(8,128)S(1)}, u32[]{:S(2)}, u32[]{:S(2)}) collective-permute-start(f32[16,224,128]{2,1,0:T(8,128)S(1)} %bitcast.15), channel_id=1, source_target_pairs={{0,1},{1,0},{2,3},{3,2},{4,5},{5,4},{6,7},{7,6},{8,9},{9,8},{10,11... | collective-permute-start | bytes 5505032 | tf_op jit(solution)/shard_map/ppermute | solution.py:362

commit v3 on v2

--- a/solution.py
+++ b/solution.py
@@ -16,6 +16,7 @@
 BF16 = jnp.bfloat16
 SLOTS = 9
 GROUP = 3
+UNROLL = 2
 OWNERS = 16
 HALF = GROUP * OWNERS
 SHARE = 224
@@ -72,8 +73,15 @@
     return row, count
 
 
-def moments_kernel(lists, list_counts, core, lw_ref, emb_ref, fac_ref, mean_ref, own_ref, other_ref,
-                   acc, tot, cnt, flipped, shift, const, rows_t, gate, items):
+def moments_kernel(place, lists_any, counts_any, lw_any, emb_any, fac_any, mean_any, own_any, other_any,
+                   acc, tot, cnt, flipped, shift, const, rows_t, gate, items,
+                   lists, list_counts, lw_ref, emb_ref, fac_ref, mean_ref, own_ref, other_ref, sems,
+                   out_sems):
+    pairs = ((lists_any, lists), (counts_any, list_counts), (lw_any, lw_ref), (emb_any, emb_ref),
+             (fac_any, fac_ref), (mean_any, mean_ref))
+    copies = [pltpu.make_async_copy(src, dst, sems.at[n]) for n, (src, dst) in enumerate(pairs)]
+    for copy in copies:
+        copy.start()
     sub = iota((8, WIDTH), 0)
     lane = iota((8, WIDTH), 1)
     ident = (iota((WIDTH, WIDTH), 0) == iota((WIDTH, WIDTH), 1)).astype(F32).astype(BF16)
@@ -83,6 +91,9 @@
     cnt[...] = jnp.zeros_like(cnt)
     gate[...] = jnp.zeros_like(gate)
     rows_t[...] = jnp.zeros_like(rows_t)
+
+    copies[0].wait()
+    copies[1].wait()
 
     def list_class(c, at):
         n = list_counts[c]
@@ -98,55 +109,66 @@
 
     total_items = lax.fori_loop(0, CLASSES, list_class, jnp.int32(0))
 
-    def half_step(i, now, before):
-        at_sum = jnp.minimum(jnp.maximum(i - 2, 0), total_items - 1)
-        at_score = jnp.minimum(jnp.maximum(i - 1, 0), total_items - 1)
-        at_class = jnp.minimum(i, total_items - 1)
-
-        c = items[0, at_sum]
-        rows = jnp.concatenate([emb_ref[items[1, at_sum]], emb_ref[items[2, at_sum]]], axis=0)
-        weights = gate[before]
-        flat = rows_t[before]
+    for copy in copies[2:]:
+        copy.wait()
+
+    def clamp(i):
+        return jnp.minimum(jnp.maximum(i, 0), total_items - 1)
+
+    def moments_of(i, u):
+        at = clamp(i)
+        c = items[0, at]
+        rows = jnp.concatenate([emb_ref[items[1, at]], emb_ref[items[2, at]]], axis=0)
+        weights = gate[u]
+        flat = rows_t[u]
         both = jnp.concatenate([rows, rows], axis=0)
-        scaled = []
         for k in range(COMPS):
             high, low = pieces(flat * weights[k : k + 1], 2)
-            scaled.append(jnp.concatenate([high, low], axis=1))
-        for k in range(COMPS):
-            acc[c * COMPS + k] += jnp.dot(scaled[k], both, preferred_element_type=F32)
+            acc[c * COMPS + k] += jnp.dot(
+                jnp.concatenate([high, low], axis=1), both, preferred_element_type=F32
+            )
         tall = jnp.concatenate([weights, jnp.zeros_like(weights)])
         sums = jnp.dot(jnp.concatenate(pieces(tall, 3)), rows, preferred_element_type=F32)
         tot[c] += sums[0:8] + sums[16:24] + sums[32:40]
         cnt[c] += weights[:, :BLOCK] + weights[:, BLOCK:]
 
-        first = emb_ref[items[1, at_score]].astype(F32).T
-        later = emb_ref[items[2, at_score]].astype(F32).T
+    def scores_of(i, u):
+        at = clamp(i)
+        first = emb_ref[items[1, at]].astype(F32).T
+        later = emb_ref[items[2, at]].astype(F32).T
         flat = jnp.concatenate([first, later], axis=1)
         square = jnp.zeros((8, 2 * BLOCK), F32)
         wide_sub = iota((8, 2 * BLOCK), 0)
         flat_half = flat.astype(BF16)
+        offsets = shift[u].astype(BF16)
+        row = iota((WIDTH, 2 * BLOCK), 0)
         for k in range(COMPS):
-            offset = shift[before, k]
-            centred = jnp.dot(flipped[before, k], flat_half, preferred_element_type=F32)
-            centred = centred - jnp.concatenate([offset, offset], axis=1)
+            ones = jnp.where((row >= 3 * k) & (row < 3 * k + 3), 1.0, 0.0).astype(BF16)
+            centred = jnp.dot(
+                jnp.concatenate([flipped[u, k], offsets], axis=1),
+                jnp.concatenate([flat_half, ones], axis=0),
+                preferred_element_type=F32,
+            )
             line = jnp.sum(centred * centred, axis=0, keepdims=True)
             square = jnp.where(wide_sub == k, line, square)
-        consts = const[before]
+        consts = const[u]
         scores = jnp.concatenate([consts, consts], axis=1) - 0.5 * square
         top = jnp.max(scores, axis=0, keepdims=True)
         weights = jnp.exp(scores - top)
         weights = weights / jnp.sum(weights, axis=0, keepdims=True)
-        live = jnp.where((i >= 1) & (i <= total_items), items[3, at_score], 0)
-        gate[now] = jnp.where(iota((8, 2 * BLOCK), 1) < live, weights, 0.0)
-        rows_t[now] = flat
-
-        c = items[0, at_class]
+        live = jnp.where((i >= 0) & (i < total_items), items[3, at], 0)
+        gate[u] = jnp.where(iota((8, 2 * BLOCK), 1) < live, weights, 0.0)
+        rows_t[u] = flat
+
+    def prepare(i, u):
+        c = items[0, clamp(i)]
         diag = jnp.ones((8, WIDTH), F32)
         prior = jnp.full((8, WIDTH), -1e30, F32)
         mean = mean_ref[:, c]
         mean_pieces = jnp.concatenate(
             pieces(jnp.concatenate([mean, jnp.zeros((16 - COMPS, WIDTH), F32)]), 3)
         )
+        lines = []
         for k in range(COMPS):
             factor = fac_ref[c, k]
             wide = factor.astype(F32)
@@ -156,21 +178,26 @@
                 on_diag = part if on_diag is None else on_diag + part
             diag = jnp.where(sub == k, jnp.sum(on_diag, axis=0, keepdims=True), diag)
             prior = jnp.where(sub == k, lw_ref[k, c], prior)
-            flipped[now, k] = wide.T.astype(BF16)
+            flipped[u, k] = wide.T.astype(BF16)
             parts = jnp.dot(mean_pieces, factor, preferred_element_type=F32)
             line = parts[k : k + 1] + parts[16 + k : 17 + k] + parts[32 + k : 33 + k]
-            shift[now, k] = jnp.broadcast_to(line, (WIDTH, WIDTH)).T
-        const[now] = jnp.sum(jnp.log(diag), axis=1, keepdims=True) + prior
-
-    def step(i, carry):
-        half_step(2 * i, 0, 1)
-        half_step(2 * i + 1, 1, 0)
+            lines += [-p.astype(F32) for p in pieces(line, 3)]
+        shift[u] = jnp.concatenate(lines + [jnp.zeros((WIDTH - 3 * COMPS, WIDTH), F32)], axis=0).T
+        const[u] = jnp.sum(jnp.log(diag), axis=1, keepdims=True) + prior
+
+    def step(j, carry):
+        for u in range(UNROLL):
+            moments_of(UNROLL * (j - 2) + u, u)
+        for u in range(UNROLL):
+            scores_of(UNROLL * (j - 1) + u, u)
+        for u in range(UNROLL):
+            prepare(UNROLL * j + u, u)
         return carry
 
-    lax.fori_loop(0, (total_items + 3) // 2, step, 0)
+    lax.fori_loop(0, (total_items + UNROLL - 1) // UNROLL + 2, step, 0)
 
     def pack(q, carry):
-        for base, out_ref in ((core[0], own_ref), (1 - core[0], other_ref)):
+        for base, out_ref in ((place[0], own_ref), (1 - place[0], other_ref)):
             for r in range(GROUP):
                 slot = base * HALF + q * GROUP + r
                 c = slot // COMPS
@@ -184,33 +211,58 @@
                 for s in range(SLOTS):
                     out_ref[q, r * ROWS + 8 * s : r * ROWS + 8 * s + 8, :] = slots[s]
             out_ref[q, GROUP * ROWS : SHARE, :] = jnp.zeros((SHARE - GROUP * ROWS, WIDTH), F32)
+        for copy in out_copies(q):
+            copy.start()
         return carry
 
+    def out_copies(q):
+        return (
+            pltpu.make_async_copy(own_ref.at[q], own_any.at[q], out_sems.at[0, q]),
+            pltpu.make_async_copy(other_ref.at[q], other_any.at[q], out_sems.at[1, q]),
+        )
+
+    def finish(q, carry):
+        for copy in out_copies(q):
+            copy.wait()
+        return carry
+
     lax.fori_loop(0, OWNERS, pack, 0)
-
-
-def local_moments(blocks, lists, list_counts, core, log_weights, factors, means):
+    lax.fori_loop(0, OWNERS, finish, 0)
+
+
+def local_moments(place, blocks, lists, list_counts, log_weights, factors, means):
     vmem = pl.BlockSpec(memory_space=pltpu.VMEM)
     smem = pl.BlockSpec(memory_space=pltpu.SMEM)
+    anywhere = pl.BlockSpec(memory_space=pltpu.HBM)
     return pl.pallas_call(
         moments_kernel,
-        in_specs=[smem, smem, smem, smem, vmem, vmem, vmem],
-        out_specs=[vmem, vmem],
+        in_specs=[smem] + [anywhere] * 6,
+        out_specs=[anywhere, anywhere],
         scratch_shapes=[
             pltpu.VMEM(((CLASSES + 1) * COMPS, WIDTH, WIDTH), F32),
             pltpu.VMEM((CLASSES + 1, 8, WIDTH), F32),
             pltpu.VMEM((CLASSES + 1, 8, WIDTH), F32),
-            pltpu.VMEM((2, COMPS, WIDTH, WIDTH), BF16),
-            pltpu.VMEM((2, COMPS, WIDTH, WIDTH), F32),
-            pltpu.VMEM((2, 8, WIDTH), F32),
-            pltpu.VMEM((2, WIDTH, 2 * BLOCK), F32),
-            pltpu.VMEM((2, 8, 2 * BLOCK), F32),
+            pltpu.VMEM((UNROLL, COMPS, WIDTH, WIDTH), BF16),
+            pltpu.VMEM((UNROLL, WIDTH, WIDTH), F32),
+            pltpu.VMEM((UNROLL, 8, WIDTH), F32),
+            pltpu.VMEM((UNROLL, WIDTH, 2 * BLOCK), F32),
+            pltpu.VMEM((UNROLL, 8, 2 * BLOCK), F32),
             pltpu.SMEM((4, 128), jnp.int32),
+            pltpu.SMEM(lists.shape, jnp.int32),
+            pltpu.SMEM(list_counts.shape, jnp.int32),
+            pltpu.SMEM(log_weights.shape, F32),
+            pltpu.VMEM(blocks.shape, BF16),
+            pltpu.VMEM(factors.shape, BF16),
+            pltpu.VMEM(means.shape, F32),
+            pltpu.VMEM((OWNERS, SHARE, WIDTH), F32),
+            pltpu.VMEM((OWNERS, SHARE, WIDTH), F32),
+            pltpu.SemaphoreType.DMA((6,)),
+            pltpu.SemaphoreType.DMA((2, OWNERS)),
         ],
         out_shape=[jax.ShapeDtypeStruct((OWNERS, SHARE, WIDTH), F32)] * 2,
-        compiler_params=pltpu.CompilerParams(vmem_limit_bytes=VMEM_LIMIT),
+        compiler_params=pltpu.CompilerParams(vmem_limit_bytes=58 * 1024 * 1024),
         name="moments",
-    )(lists, list_counts, core, log_weights, blocks, factors, means)
+    )(place, lists, list_counts, log_weights, blocks, factors, means)
 
 
 def solve_kernel(place, mine_ref, theirs_ref, mean_ref, out_ref):
@@ -233,58 +285,76 @@
         old_t = jnp.broadcast_to(old, (WIDTH, WIDTH)).T
         new_t = jnp.broadcast_to(new * denom, (WIDTH, WIDTH)).T
         second = unpack_strips(slots)
+        full = jnp.concatenate(second, axis=0)
+        mirror = full.T
         rows = []
         for s in range(STRIPS):
             cut = slice(8 * s, 8 * s + 8)
-            scatter = second[s] + old_t[cut] * old - new_t[cut] * new
+            scatter = jnp.where(lane >= 8 * s, second[s], mirror[cut])
+            scatter = scatter + old_t[cut] * old - new_t[cut] * new
             scatter = jnp.where(lane - 8 * s == sub, scatter + 1.0, scatter)
-            rows.append(jnp.where(lane >= 8 * s, scatter / denom, 0.0))
+            rows.append(scatter / denom)
         strips.append(rows)
         new_means.append(new)
         counts.append(count)
     for s in range(STRIPS):
         for g in range(GROUP):
             rows = strips[g]
+            block = (lane >= 8 * s) & (lane < 8 * s + 8)
             panel = rows[s]
             columns = [
                 jnp.broadcast_to(panel[:, 8 * s + j : 8 * s + j + 1], (8, WIDTH)) for j in range(8)
             ]
-            block = (lane >= 8 * s) & (lane < 8 * s + 8)
             panel = jnp.where(block, jnp.where(lane - 8 * s == sub, 1.0, 0.0), panel)
+            ahead = s + 1 < STRIPS
+            if ahead:
+                after = rows[s + 1]
+                behind = [
+                    jnp.broadcast_to(after[:, 8 * s + j : 8 * s + j + 1], (8, WIDTH))
+                    for j in range(8)
+                ]
+                after = jnp.where(block, 0.0, after)
             pivots = jnp.ones((8, WIDTH), F32)
             for j in range(8):
                 pivot = columns[j][j : j + 1]
+                inverse = 1.0 / pivot
                 pivots = jnp.where(sub == j, pivot, pivots)
+                line = panel[j : j + 1]
+                if ahead:
+                    ratio = behind[j] * inverse
+                    after = after - ratio * line
+                    for l in range(j + 1, 8):
+                        behind[l] = behind[l] - ratio * columns[l][j : j + 1]
                 if j < 7:
-                    ratio = jnp.where(sub > j, columns[j] * (1.0 / pivot), 0.0)
-                    panel = panel - ratio * panel[j : j + 1]
+                    ratio = jnp.where(sub > j, columns[j] * inverse, 0.0)
+                    panel = panel - ratio * line
                     for l in range(j + 1, 8):
                         columns[l] = columns[l] - ratio * columns[l][j : j + 1]
             panel = panel * (1.0 / jnp.sqrt(pivots))
             rows[s] = panel
-            if s < STRIPS - 1:
+            if ahead:
+                rows[s + 1] = after
+            if s + 2 < STRIPS:
                 a, b, d = [p.astype(F32) for p in pieces(panel, 3)]
                 left = jnp.concatenate([a, a, b, b, a, d], axis=0).astype(BF16)
                 right = jnp.concatenate([a, b, a, b, d, a], axis=0).astype(BF16)
                 change = lax.dot_general(
                     left, right, (((0,), (0,)), ((), ())), preferred_element_type=F32
                 )
-                for t in range(s + 1, STRIPS):
+                for t in range(s + 2, STRIPS):
                     base = jnp.where(block, 0.0, rows[t])
                     rows[t] = base - change[8 * t : 8 * t + 8]
-    packed = []
     for g in range(GROUP):
         lower = jnp.concatenate(
             [jnp.where(lane - 8 * s <= sub, strips[g][s], 0.0) for s in range(STRIPS)], axis=0
         )
         upper = lower.T
-        packed += pack_strips(
+        slots = pack_strips(
             [upper[8 * s : 8 * s + 8] for s in range(STRIPS)],
             extra_rows(new_means[g], counts[g]),
         )
-    packed.append(jnp.zeros((8, WIDTH), F32))
-    for t in range(PART // 8):
-        out_ref[8 * t : 8 * t + 8, :] = jnp.where(early, packed[t], packed[PART // 8 + t])
+        for s in range(SLOTS):
+            out_ref[g * ROWS + 8 * s : g * ROWS + 8 * s + 8, :] = slots[s]
 
 
 def solve_share(place, mine, theirs, means):
@@ -294,7 +364,7 @@
         solve_kernel,
         in_specs=[smem, vmem, vmem, vmem],
         out_specs=vmem,
-        out_shape=jax.ShapeDtypeStruct((PART, WIDTH), F32),
+        out_shape=jax.ShapeDtypeStruct((GROUP * ROWS, WIDTH), F32),
         compiler_params=pltpu.CompilerParams(vmem_limit_bytes=VMEM_LIMIT),
         name="solve",
     )(place, mine, theirs, means)
@@ -303,7 +373,7 @@
 UNPACK = 19
 
 
-def unpack_kernel(core, here_ref, there_ref, factor_ref, mean_ref, log_ref, counts):
+def unpack_kernel(place, here_ref, there_ref, factor_ref, mean_ref, log_ref, counts):
     step = pl.program_id(0)
     for g in range(UNPACK):
         comp = step * UNPACK + g
@@ -311,7 +381,7 @@
         at = comp - half * HALF
         q = at // GROUP
         first = pl.multiple_of((at - q * GROUP) * ROWS, 8)
-        here = half == core[0]
+        here = half == place[0]
         slots = []
         for s in range(SLOTS):
             cut = pl.ds(first + 8 * s, 8)
@@ -335,7 +405,7 @@
             log_ref[k : k + 1, :] = jnp.sum(logs, axis=0, keepdims=True)[:, :CLASSES]
 
 
-def unpack_all(core, here, there):
+def unpack_all(place, here, there):
     steps = CLASSES * COMPS // UNPACK
     vmem = pl.BlockSpec(memory_space=pltpu.VMEM)
     return pl.pallas_call(
@@ -355,7 +425,7 @@
         scratch_shapes=[pltpu.VMEM((COMPS, CLASSES, WIDTH), F32)],
         compiler_params=pltpu.CompilerParams(vmem_limit_bytes=VMEM_LIMIT),
         name="unpack",
-    )(core, here, there)
+    )(place, here, there)
 
 
 def swap_cores(value):
@@ -373,23 +443,26 @@
     frames_here, pixels_here, width = embeddings.shape
     blocks = embeddings.reshape(frames_here * pixels_here // BLOCK, BLOCK, width)
     core = lax.axis_index("core").astype(jnp.int32)
-    near = lax.axis_index("near").astype(jnp.int32)
+    late = lax.axis_index("near").astype(jnp.int32)
     owner = (lax.axis_index("x") * 4 + lax.axis_index("y")).astype(jnp.int32)
     means_t = jnp.transpose(means, (1, 0, 2))
+    place = core[None]
     own, other = local_moments(
-        blocks, class_blocks[0, 0].T, class_counts[0, 0], core[None], log_weights.T, factors, means_t
+        place, blocks, class_blocks[0, 0].T, class_counts[0, 0], log_weights.T, factors, means_t
     )
     peers = ("x", "y", "near")
     half = own + swap_cores(other)
     parts = lax.all_to_all(half.reshape(2 * OWNERS, PART, width), peers, 0, 0, tiled=True)
-    mine = sum_far(jnp.sum(parts, axis=0))
+    mine = jnp.sum(parts, axis=0)
+    mine = sum_far(mine)
     theirs = lax.ppermute(mine, "near", [(0, 1), (1, 0)])
-    place = jnp.stack([core * HALF + owner * GROUP, near])
-    solved = solve_share(place, mine, theirs, means_t)
-    spread = jnp.broadcast_to(solved[None], (2 * OWNERS, PART, width))
-    here = lax.all_to_all(spread, peers, 0, 0, tiled=True).reshape(OWNERS, SHARE, width)
+    solved = solve_share(
+        jnp.stack([core * HALF + owner * GROUP, late]), mine, theirs, means_t
+    )
+    spread = jnp.broadcast_to(solved[None], (OWNERS,) + solved.shape)
+    here = lax.all_to_all(spread, ("x", "y"), 0, 0, tiled=True)
     there = swap_cores(here)
-    new_factor, new_mean, new_log = unpack_all(core[None], here, there)
+    new_factor, new_mean, new_log = unpack_all(place, here, there)
     return (
         new_log.T,
         jnp.transpose(new_mean, (1, 0, 2)),

time: 124 us -> 117 us (0.944)
  local copies, waits for them, and re-layouts: 4.2 us -> 0.12 us
  Pallas kernels: 29 us -> 25.7 us
  waiting for transfers between devices: 15.2 us -> 13.5 us
  blocking collectives: 56.5 us -> 54.9 us
  other arithmetic: 0.44 us -> 1.92 us
  starting transfers between devices: 18 us -> 19.4 us
    unnamed x12 -> x2, local copies, waits for them, and re-layouts: 4.08 us -> 0.01 us
    pallas_call x1, Pallas kernels: 17.6 us -> 15.4 us  [local_moments(): pl.pallas_call(moments_kernel, in_specs=[smem] + [anywhere] * 6, out_spec...]
    all_to_all x1, blocking collectives: 24.9 us -> 23.2 us  [body(): here = lax.all_to_all(spread, ('x', 'y'), 0, 0, tiled=True)]
    add x1, other arithmetic: 0.26 us -> 1.73 us  [body(): half = own + swap_cores(other)]
where the time goes in v3:
time: 117 us; the launch traced here: 116 us
  blocking collectives  54.9 us (47%)
  Pallas kernels  25.7 us (22%)
  starting transfers between devices  19.4 us (17%)
  waiting for transfers between devices  13.5 us (12%)
  other arithmetic  1.92 us (2%)
    all_to_all x1, blocking collectives, body(): lax.all_to_all(half.reshape(2 * OWNERS, PART, width), peers, 0, 0, tiled=...  31.7 us
    all_to_all x1, blocking collectives, body(): here = lax.all_to_all(spread, ('x', 'y'), 0, 0, tiled=True)  23.2 us
    pallas_call x1, Pallas kernels, local_moments(): pl.pallas_call(moments_kernel, in_specs=[smem] + [anywhere] * 6, out_spec...  15.4 us
    ppermute x2, starting transfers between devices, swap_cores(): return lax.ppermute(value, 'core', [(0, 1), (1, 0)])  10.4 us
    ppermute x3, starting transfers between devices, sum_far(): lax.ppermute(value, 'far', [(i, (i + hop) % 4) for i in range(4)])  8.25 us
    ppermute x2, waiting for transfers between devices, swap_cores(): return lax.ppermute(value, 'core', [(0, 1), (1, 0)])  6.94 us
    pallas_call x1, Pallas kernels, solve_share(): pl.pallas_call(solve_kernel, in_specs=[smem, vmem, vmem, vmem], out_specs...  6.08 us
    pallas_call x1, Pallas kernels, unpack_all(): pl.pallas_call(unpack_kernel, grid=(steps,), in_specs=[pl.BlockSpec(memor...  4.27 us
  transfers between devices with their start and end apart: 6, of which 5 were waited for; matrix products, arithmetic and copies ran while one was open for 0% of the time, Pallas kernels for 0%

profile of v3, /device:TPU:1, one launch (start us, length us, event | category | flops | bytes accessed | tf_op | source)
XLA Modules:
  0.0 116.2 jit_solution(846395780366562378)
XLA Ops:
  0.6 15.4 %moments.1 = (f32[16,224,128]{2,1,0:T(8,128)}, f32[16,224,128]{2,1,0:T(8,128)}) custom-call(s32[1]{0:T(128)} %bitcast.place, s32[8,19]{1,0:T(8,128)} %bitcast.18, s32[19]{0:T(128)} %bitcast.20, f32[5,19]{1,0:T(8,128)} %bitcast.19, bf16[32,128,128]{2,1,0:T(8,128)(2,1)} %bitcast.17, bf16[19,5,128,128]{3,2,1,0:T(8,128)(2,1)} %fac_any.1, f32[5,19,128]{2,1,0:T(8,128)} %bitcast.14), custom_call_target="tpu_custom_call" | custom-call | tf_op jit(solution)/shard_map/moments/pallas_call | solution.py:237
  16.0 5.2 %collective-permute-start = (f32[16,224,128]{2,1,0:T(8,128)}, f32[16,224,128]{2,1,0:T(8,128)S(1)}, u32[]{:S(2)}, u32[]{:S(2)}) collective-permute-start(f32[16,224,128]{2,1,0:T(8,128)} %get-tuple-element.9), channel_id=1, source_target_pairs={{0,1},{1,0},{2,3},{3,2},{4,5},{5,4},{6,7},{7,6},{8,9},{9,8},{10,11... | collective-permute-start | bytes 5505032 | tf_op jit(solution)/shard_map/ppermute | solution.py:432
  21.2 3.6 %collective-permute-done = f32[16,224,128]{2,1,0:T(8,128)S(1)} collective-permute-done((f32[16,224,128]{2,1,0:T(8,128)}, f32[16,224,128]{2,1,0:T(8,128)S(1)}, u32[]{:S(2)}, u32[]{:S(2)}) %collective-permute-start) | collective-permute-done | bytes 1835040 | tf_op jit(solution)/shard_map/ppermute | solution.py:432
  24.8 1.7 %add.20 = f32[16,224,128]{2,1,0:T(8,128)S(1)} add(f32[16,224,128]{2,1,0:T(8,128)} %get-tuple-element.8, f32[16,224,128]{2,1,0:T(8,128)S(1)} %collective-permute-done) | non-fusion elementwise | flops 458752 | bytes 5505024 | tf_op jit(solution)/shard_map/add | solution.py:454
  26.6 31.7 %all_to_all.10 = f32[32,112,128]{2,1,0:T(8,128)S(1)} all-to-all(f32[32,112,128]{2,1,0:T(8,128)S(1)} %bitcast.16), channel_id=1, replica_groups=mesh['x'=4,'far'=4,'near'=2,'y'=4,'core'=2] {'x','y','near'}, dimensions={0} | all-to-all | bytes 3670016 | tf_op jit(solution)/shard_map/all_to_all | solution.py:455
  58.2 0.0 copy-start
  58.3 0.1 reduce_sum.9
  58.4 4.8 %collective-permute-start.3 = (f32[112,128]{1,0:T(8,128)S(1)}, f32[112,128]{1,0:T(8,128)S(1)}, u32[]{:S(2)}, u32[]{:S(2)}) collective-permute-start(f32[112,128]{1,0:T(8,128)S(1)} %reduce_sum.9), channel_id=1, source_target_pairs={{0,48},{16,0},{32,16},{48,32},{1,49},{17,1},{33,17},{49,33},{2,50}... | collective-permute-start | bytes 172040 | tf_op jit(solution)/shard_map/ppermute | solution.py:438
  63.2 0.0 collective-permute-start.2
  63.2 3.4 %collective-permute-start.1 = (f32[112,128]{1,0:T(8,128)S(1)}, f32[112,128]{1,0:T(8,128)S(1)}, u32[]{:S(2)}, u32[]{:S(2)}) collective-permute-start(f32[112,128]{1,0:T(8,128)S(1)} %reduce_sum.9), channel_id=1, source_target_pairs={{0,32},{16,48},{32,0},{48,16},{1,33},{17,49},{33,1},{49,17},{2,34}... | collective-permute-start | bytes 172040 | tf_op jit(solution)/shard_map/ppermute | solution.py:438
  66.6 0.0 collective-permute-done.3
  66.6 1.7 %collective-permute-done.2 = f32[112,128]{1,0:T(8,128)S(1)} collective-permute-done((f32[112,128]{1,0:T(8,128)S(1)}, f32[112,128]{1,0:T(8,128)S(1)}, u32[]{:S(2)}, u32[]{:S(2)}) %collective-permute-start.2) | collective-permute-done | bytes 57376 | tf_op jit(solution)/shard_map/ppermute | solution.py:438
  68.3 2.0 %collective-permute-done.1 = f32[112,128]{1,0:T(8,128)S(1)} collective-permute-done((f32[112,128]{1,0:T(8,128)S(1)}, f32[112,128]{1,0:T(8,128)S(1)}, u32[]{:S(2)}, u32[]{:S(2)}) %collective-permute-start.1) | collective-permute-done | bytes 57376 | tf_op jit(solution)/shard_map/ppermute | solution.py:438
  70.4 0.7 collective-permute-start.4
  71.1 0.1 pad_add_fusion.place
  71.1 2.8 %collective-permute-done.4.theirs_ref = f32[112,128]{1,0:T(8,128)S(1)} collective-permute-done((f32[112,128]{1,0:T(8,128)S(1)}, f32[112,128]{1,0:T(8,128)S(1)}, u32[]{:S(2)}, u32[]{:S(2)}) %collective-permute-start.4) | collective-permute-done | bytes 57376 | tf_op jit(solution)/shard_map/ppermute | solution.py:458
  73.9 0.0 copy-done
  73.9 6.1 %solve.1 = f32[216,128]{1,0:T(8,128)S(1)} custom-call(s32[2]{0:T(128)S(1)} %pad_add_fusion.place, f32[112,128]{1,0:T(8,128)S(1)} %add_add_fusion.mine_ref, f32[112,128]{1,0:T(8,128)S(1)} %collective-permute-done.4.theirs_ref, f32[5,19,128]{2,1,0:T(8,128)S(1)} %bitcast.15), custom_call_target="tpu_custom_call" | custom-call | tf_op jit(solution)/shard_map/solve/pallas_call | solution.py:363
  80.0 0.1 broadcast_in_dim.10
  80.2 23.2 %all_to_all.11.here_ref = f32[16,216,128]{2,1,0:T(8,128)S(1)} all-to-all(f32[16,216,128]{2,1,0:T(8,128)S(1)} %broadcast_in_dim.10), channel_id=1, replica_groups=mesh['x'=4,'far'=4,'near'=2,'y'=4,'core'=2] {'x','y'}, dimensions={0} | all-to-all | bytes 3538944 | tf_op jit(solution)/shard_map/all_to_all | solution.py:463
  103.4 5.2 %collective-permute-start.5 = (f32[16,216,128]{2,1,0:T(8,128)S(1)}, f32[16,216,128]{2,1,0:T(8,128)S(1)}, u32[]{:S(2)}, u32[]{:S(2)}) collective-permute-start(f32[16,216,128]{2,1,0:T(8,128)S(1)} %all_to_all.11.here_ref), channel_id=1, source_target_pairs={{0,1},{1,0},{2,3},{3,2},{4,5},{5,4},{6,7},{7,6},{8,9},{9,8},{10,11... | collective-permute-start | bytes 5308424 | tf_op jit(solution)/shard_map/ppermute | solution.py:432
  108.6 3.3 %collective-permute-done.5.there_ref = f32[16,216,128]{2,1,0:T(8,128)S(1)} collective-permute-done((f32[16,216,128]{2,1,0:T(8,128)S(1)}, f32[16,216,128]{2,1,0:T(8,128)S(1)}, u32[]{:S(2)}, u32[]{:S(2)}) %collective-permute-start.5) | collective-permute-done | bytes 1769504 | tf_op jit(solution)/shard_map/ppermute | solution.py:432
  111.9 4.3 %unpack.1 = (f32[95,128,128]{2,1,0:T(8,128)}, f32[5,19,128]{2,1,0:T(8,128)}, f32[5,19]{1,0:T(8,128)}) custom-call(s32[1]{0:T(128)} %bitcast.place, f32[16,216,128]{2,1,0:T(8,128)S(1)} %all_to_all.11.here_ref, f32[16,216,128]{2,1,0:T(8,128)S(1)} %collective-permute-done.5.there_ref), custom_call_target="tpu_custom_call" | custom-call | tf_op jit(solution)/shard_map/unpack/pallas_call | solution.py:411
  (1 shorter events, 0.0 us)
Async XLA Ops:
  16.0 8.8 %collective-permute-start = (f32[16,224,128]{2,1,0:T(8,128)}, f32[16,224,128]{2,1,0:T(8,128)S(1)}, u32[]{:S(2)}, u32[]{:S(2)}) collective-permute-start(f32[16,224,128]{2,1,0:T(8,128)} %get-tuple-element.9), channel_id=1, source_target_pairs={{0,1},{1,0},{2,3},{3,2},{4,5},{5,4},{6,7},{7,6},{8,9},{9,8},{10,11... | collective-permute-start | bytes 5505032 | tf_op jit(solution)/shard_map/ppermute | solution.py:432
  58.2 15.7 %copy-start = (f32[19,5,128]{2,0,1:T(8,128)S(1)}, f32[19,5,128]{2,0,1:T(8,128)}, u32[]{:S(2)}) copy-start(f32[19,5,128]{2,0,1:T(8,128)} %param.9) | copy-start | bytes 145924
  58.4 8.3 %collective-permute-start.3 = (f32[112,128]{1,0:T(8,128)S(1)}, f32[112,128]{1,0:T(8,128)S(1)}, u32[]{:S(2)}, u32[]{:S(2)}) collective-permute-start(f32[112,128]{1,0:T(8,128)S(1)} %reduce_sum.9), channel_id=1, source_target_pairs={{0,48},{16,0},{32,16},{48,32},{1,49},{17,1},{33,17},{49,33},{2,50}... | collective-permute-start | bytes 172040 | tf_op jit(solution)/shard_map/ppermute | solution.py:438
  63.2 5.1 %collective-permute-start.2 = (f32[112,128]{1,0:T(8,128)S(1)}, f32[112,128]{1,0:T(8,128)S(1)}, u32[]{:S(2)}, u32[]{:S(2)}) collective-permute-start(f32[112,128]{1,0:T(8,128)S(1)} %reduce_sum.9), channel_id=1, source_target_pairs={{0,16},{16,32},{32,48},{48,0},{1,17},{17,33},{33,49},{49,1},{2,18}... | collective-permute-start | bytes 172040 | tf_op jit(solution)/shard_map/ppermute | solution.py:438
  63.2 7.2 %collective-permute-start.1 = (f32[112,128]{1,0:T(8,128)S(1)}, f32[112,128]{1,0:T(8,128)S(1)}, u32[]{:S(2)}, u32[]{:S(2)}) collective-permute-start(f32[112,128]{1,0:T(8,128)S(1)} %reduce_sum.9), channel_id=1, source_target_pairs={{0,32},{16,48},{32,0},{48,16},{1,33},{17,49},{33,1},{49,17},{2,34}... | collective-permute-start | bytes 172040 | tf_op jit(solution)/shard_map/ppermute | solution.py:438
  70.4 3.6 %collective-permute-start.4 = (f32[112,128]{1,0:T(8,128)S(1)}, f32[112,128]{1,0:T(8,128)S(1)}, u32[]{:S(2)}, u32[]{:S(2)}) collective-permute-start(f32[112,128]{1,0:T(8,128)S(1)} %add_add_fusion.mine_ref), channel_id=1, source_target_pairs={{0,8},{8,0},{1,9},{9,1},{2,10},{10,2},{3,11},{11,3},{4,12},{12,4},... | collective-permute-start | bytes 172040 | tf_op jit(solution)/shard_map/ppermute | solution.py:458
  103.4 8.6 %collective-permute-start.5 = (f32[16,216,128]{2,1,0:T(8,128)S(1)}, f32[16,216,128]{2,1,0:T(8,128)S(1)}, u32[]{:S(2)}, u32[]{:S(2)}) collective-permute-start(f32[16,216,128]{2,1,0:T(8,128)S(1)} %all_to_all.11.here_ref), channel_id=1, source_target_pairs={{0,1},{1,0},{2,3},{3,2},{4,5},{5,4},{6,7},{7,6},{8,9},{9,8},{10,11... | collective-permute-start | bytes 5308424 | tf_op jit(solution)/shard_map/ppermute | solution.py:432

commit v4 on v3

--- a/solution.py
+++ b/solution.py
@@ -73,10 +73,9 @@
     return row, count
 
 
-def moments_kernel(place, lists_any, counts_any, lw_any, emb_any, fac_any, mean_any, own_any, other_any,
+def moments_kernel(place, lists_any, counts_any, lw_any, emb_any, fac_any, mean_any, own_ref, other_ref,
                    acc, tot, cnt, flipped, shift, const, rows_t, gate, items,
-                   lists, list_counts, lw_ref, emb_ref, fac_ref, mean_ref, own_ref, other_ref, sems,
-                   out_sems):
+                   lists, list_counts, lw_ref, emb_ref, fac_ref, mean_ref, sems):
     pairs = ((lists_any, lists), (counts_any, list_counts), (lw_any, lw_ref), (emb_any, emb_ref),
              (fac_any, fac_ref), (mean_any, mean_ref))
     copies = [pltpu.make_async_copy(src, dst, sems.at[n]) for n, (src, dst) in enumerate(pairs)]
@@ -211,23 +210,9 @@
                 for s in range(SLOTS):
                     out_ref[q, r * ROWS + 8 * s : r * ROWS + 8 * s + 8, :] = slots[s]
             out_ref[q, GROUP * ROWS : SHARE, :] = jnp.zeros((SHARE - GROUP * ROWS, WIDTH), F32)
-        for copy in out_copies(q):
-            copy.start()
         return carry
 
-    def out_copies(q):
-        return (
-            pltpu.make_async_copy(own_ref.at[q], own_any.at[q], out_sems.at[0, q]),
-            pltpu.make_async_copy(other_ref.at[q], other_any.at[q], out_sems.at[1, q]),
-        )
-
-    def finish(q, carry):
-        for copy in out_copies(q):
-            copy.wait()
-        return carry
-
     lax.fori_loop(0, OWNERS, pack, 0)
-    lax.fori_loop(0, OWNERS, finish, 0)
 
 
 def local_moments(place, blocks, lists, list_counts, log_weights, factors, means):
@@ -237,7 +222,7 @@
     return pl.pallas_call(
         moments_kernel,
         in_specs=[smem] + [anywhere] * 6,
-        out_specs=[anywhere, anywhere],
+        out_specs=[vmem, vmem],
         scratch_shapes=[
             pltpu.VMEM(((CLASSES + 1) * COMPS, WIDTH, WIDTH), F32),
             pltpu.VMEM((CLASSES + 1, 8, WIDTH), F32),
@@ -254,15 +239,12 @@
             pltpu.VMEM(blocks.shape, BF16),
             pltpu.VMEM(factors.shape, BF16),
             pltpu.VMEM(means.shape, F32),
-            pltpu.VMEM((OWNERS, SHARE, WIDTH), F32),
-            pltpu.VMEM((OWNERS, SHARE, WIDTH), F32),
             pltpu.SemaphoreType.DMA((6,)),
-            pltpu.SemaphoreType.DMA((2, OWNERS)),
         ],
         out_shape=[jax.ShapeDtypeStruct((OWNERS, SHARE, WIDTH), F32)] * 2,
-        compiler_params=pltpu.CompilerParams(vmem_limit_bytes=58 * 1024 * 1024),
+        compiler_params=pltpu.CompilerParams(vmem_limit_bytes=VMEM_LIMIT),
         name="moments",
-    )(place, lists, list_counts, log_weights, blocks, factors, means)
+    )(place, *[pltpu.with_memory_space_constraint(v, pltpu.HBM) for v in (lists, list_counts, log_weights, blocks, factors, means)])
 
 
 def solve_kernel(place, mine_ref, theirs_ref, mean_ref, out_ref):
@@ -370,62 +352,101 @@
     )(place, mine, theirs, means)
 
 
-UNPACK = 19
-
-
-def unpack_kernel(place, here_ref, there_ref, factor_ref, mean_ref, log_ref, counts):
-    step = pl.program_id(0)
-    for g in range(UNPACK):
-        comp = step * UNPACK + g
-        half = jnp.where(comp >= HALF, 1, 0)
-        at = comp - half * HALF
-        q = at // GROUP
-        first = pl.multiple_of((at - q * GROUP) * ROWS, 8)
-        here = half == place[0]
-        slots = []
-        for s in range(SLOTS):
-            cut = pl.ds(first + 8 * s, 8)
-            slots.append(jnp.where(here, here_ref[q, cut, :], there_ref[q, cut, :]))
-        strips = unpack_strips(slots)
-        for s in range(STRIPS):
-            factor_ref[g, 8 * s : 8 * s + 8, :] = strips[s]
-        row, count = split_extra(slots[8])
-        c = comp // COMPS
-        k = comp - c * COMPS
-        mean_ref[k, pl.ds(c, 1), :] = row
-        counts[k, pl.ds(c, 1), :] = count
-
-    @pl.when(step == CLASSES * COMPS // UNPACK - 1)
-    def _():
-        mask = iota((CLASSES, WIDTH), 0) == iota((CLASSES, WIDTH), 1)
-        values = [counts[k] for k in range(COMPS)]
-        total = jnp.log(sum(values) + float(COMPS))
-        for k in range(COMPS):
-            logs = jnp.where(mask, jnp.log(values[k] + 1.0) - total, 0.0)
-            log_ref[k : k + 1, :] = jnp.sum(logs, axis=0, keepdims=True)[:, :CLASSES]
-
-
-def unpack_all(place, here, there):
-    steps = CLASSES * COMPS // UNPACK
+def unpack_half(half, part_ref, factor_any, mean_ref, counts, buffer, sems):
+    def copy_of(at):
+        comp = half * HALF + at
+        copy = pltpu.make_async_copy(buffer.at[at], factor_any.at[comp], sems.at[at])
+        return comp < CLASSES * COMPS, copy
+
+    def unpack(q, carry):
+        for r in range(GROUP):
+            at = q * GROUP + r
+            comp = half * HALF + at
+            slots = [part_ref[q, r * ROWS + 8 * s : r * ROWS + 8 * s + 8, :] for s in range(SLOTS)]
+            strips = unpack_strips(slots)
+            for s in range(STRIPS):
+                buffer[at, 8 * s : 8 * s + 8, :] = strips[s]
+            row, count = split_extra(slots[8])
+            c = jnp.minimum(comp // COMPS, CLASSES)
+            k = comp - comp // COMPS * COMPS
+            mean_ref[k, pl.ds(c, 1), :] = row
+            counts[k, pl.ds(c, 1), :] = count
+        for r in range(GROUP):
+            real, copy = copy_of(q * GROUP + r)
+            pl.when(real)(copy.start)
+        return carry
+
+    def finish(at, carry):
+        real, copy = copy_of(at)
+        pl.when(real)(copy.wait)
+        return carry
+
+    lax.fori_loop(0, OWNERS, unpack, 0)
+    return finish
+
+
+def unpack_first_kernel(place, part_ref, factor_any, mean_ref, count_ref, buffer, sems):
+    finish = unpack_half(place[0], part_ref, factor_any, mean_ref, count_ref, buffer, sems)
+    lax.fori_loop(0, HALF, finish, 0)
+
+
+def unpack_last_kernel(place, part_ref, begun_any, mean_part, count_part, factor_any, mean_ref, log_ref,
+                       means, counts, buffer, sems):
+    half = 1 - place[0]
+    finish = unpack_half(half, part_ref, factor_any, means, counts, buffer, sems)
+    comp = iota((PADDED, WIDTH), 0) * COMPS
+    values = []
+    for k in range(COMPS):
+        here = (comp + k >= HALF) == (half == 1)
+        mean_ref[k] = jnp.where(here, means[k], mean_part[k])[:CLASSES]
+        values.append(jnp.where(here, counts[k], count_part[k])[:CLASSES])
+    mask = iota((CLASSES, WIDTH), 0) == iota((CLASSES, WIDTH), 1)
+    total = jnp.log(sum(values) + float(COMPS))
+    for k in range(COMPS):
+        logs = jnp.where(mask, jnp.log(values[k] + 1.0) - total, 0.0)
+        log_ref[k : k + 1, :] = jnp.sum(logs, axis=0, keepdims=True)[:, :CLASSES]
+    lax.fori_loop(0, HALF, finish, 0)
+
+
+PADDED = 24
+
+
+def unpack_all(place, here, there_of):
     vmem = pl.BlockSpec(memory_space=pltpu.VMEM)
+    smem = pl.BlockSpec(memory_space=pltpu.SMEM)
+    hbm = pl.BlockSpec(memory_space=pltpu.HBM)
+    factor = jax.ShapeDtypeStruct((CLASSES * COMPS, WIDTH, WIDTH), F32)
+    part = jax.ShapeDtypeStruct((COMPS, PADDED, WIDTH), F32)
+    work = [pltpu.VMEM((HALF, WIDTH, WIDTH), F32), pltpu.SemaphoreType.DMA((HALF,))]
+    rows = pltpu.VMEM(part.shape, F32)
+    cost = pl.CostEstimate(flops=4000000, bytes_accessed=5000000, transcendentals=0)
+    params = pltpu.CompilerParams(vmem_limit_bytes=VMEM_LIMIT)
+    there = there_of(here)
+    begun, mean_part, count_part = pl.pallas_call(
+        unpack_first_kernel,
+        in_specs=[smem, vmem],
+        out_specs=[hbm, vmem, vmem],
+        out_shape=[factor, part, part],
+        scratch_shapes=work,
+        compiler_params=params,
+        cost_estimate=cost,
+        name="unpack_first",
+    )(place, here)
     return pl.pallas_call(
-        unpack_kernel,
-        grid=(steps,),
-        in_specs=[pl.BlockSpec(memory_space=pltpu.SMEM), vmem, vmem],
-        out_specs=[
-            pl.BlockSpec((UNPACK, WIDTH, WIDTH), lambda i: (i, 0, 0)),
-            pl.BlockSpec((COMPS, CLASSES, WIDTH), lambda i: (0, 0, 0)),
-            pl.BlockSpec((COMPS, CLASSES), lambda i: (0, 0)),
-        ],
+        unpack_last_kernel,
+        in_specs=[smem, vmem, hbm, vmem, vmem],
+        out_specs=[hbm, vmem, vmem],
         out_shape=[
-            jax.ShapeDtypeStruct((CLASSES * COMPS, WIDTH, WIDTH), F32),
+            factor,
             jax.ShapeDtypeStruct((COMPS, CLASSES, WIDTH), F32),
             jax.ShapeDtypeStruct((COMPS, CLASSES), F32),
         ],
-        scratch_shapes=[pltpu.VMEM((COMPS, CLASSES, WIDTH), F32)],
-        compiler_params=pltpu.CompilerParams(vmem_limit_bytes=VMEM_LIMIT),
-        name="unpack",
-    )(place, here, there)
+        input_output_aliases={2: 0},
+        scratch_shapes=[rows, rows] + work,
+        compiler_params=params,
+        cost_estimate=cost,
+        name="unpack_last",
+    )(place, there, begun, mean_part, count_part)
 
 
 def swap_cores(value):
@@ -461,8 +482,7 @@
     )
     spread = jnp.broadcast_to(solved[None], (OWNERS,) + solved.shape)
     here = lax.all_to_all(spread, ("x", "y"), 0, 0, tiled=True)
-    there = swap_cores(here)
-    new_factor, new_mean, new_log = unpack_all(place, here, there)
+    new_factor, new_mean, new_log = unpack_all(place, here, swap_cores)
     return (
         new_log.T,
         jnp.transpose(new_mean, (1, 0, 2)),

time: 117 us -> 113 us (0.966)
  waiting for transfers between devices: 13.5 us -> 10.4 us
  Pallas kernels: 25.7 us -> 27.4 us
  other arithmetic: 1.92 us -> 0.47 us
    ppermute x2, waiting for transfers between devices: 6.94 us -> 4.09 us  [swap_cores(): return lax.ppermute(value, 'core', [(0, 1), (1, 0)])]
    pallas_call x1 -> x2, Pallas kernels: 4.27 us -> 5.92 us  [the longest x1 3.28 us: unpack_all(): pl.pallas_call(unpack_last_kernel, in_specs=[smem, vmem, hbm, vmem, vmem]...]
    add x1, other arithmetic: 1.73 us -> 0.28 us  [body(): half = own + swap_cores(other)]
  transfers between devices with their start and end apart: 6 -> 6, of which waited for: 5 -> 5; matrix products, arithmetic and copies ran while one was open for 0% -> 0% of each run, Pallas kernels for 0% -> 2%
where the time goes in v4:
time: 113 us
  blocking collectives  54.9 us (49%)
  Pallas kernels  27.4 us (24%)
  starting transfers between devices  19.2 us (17%)
  waiting for transfers between devices  10.4 us (9%)
    all_to_all x1, blocking collectives, body(): lax.all_to_all(half.reshape(2 * OWNERS, PART, width), peers, 0, 0, tiled=...  32.4 us
    all_to_all x1, blocking collectives, body(): here = lax.all_to_all(spread, ('x', 'y'), 0, 0, tiled=True)  22.4 us
    pallas_call x1, Pallas kernels, local_moments(): pl.pallas_call(moments_kernel, in_specs=[smem] + [anywhere] * 6, out_spec...  15.4 us
    ppermute x2, starting transfers between devices, swap_cores(): return lax.ppermute(value, 'core', [(0, 1), (1, 0)])  10 us
    ppermute x3, starting transfers between devices, sum_far(): lax.ppermute(value, 'far', [(i, (i + hop) % 4) for i in range(4)])  8.89 us
    pallas_call x1, Pallas kernels, solve_share(): pl.pallas_call(solve_kernel, in_specs=[smem, vmem, vmem, vmem], out_specs...  6.08 us
    ppermute x2, waiting for transfers between devices, swap_cores(): return lax.ppermute(value, 'core', [(0, 1), (1, 0)])  4.09 us
    ppermute x1, waiting for transfers between devices, body(): theirs = lax.ppermute(mine, 'near', [(0, 1), (1, 0)])  3.34 us
  transfers between devices with their start and end apart: 6, of which 5 were waited for; matrix products, arithmetic and copies ran while one was open for 0% of the time, Pallas kernels for 2%

profile of v4, /device:TPU:1, one launch (start us, length us, event | category | flops | bytes accessed | tf_op | source)
XLA Modules:
  0.0 113.1 jit_solution(11057082919505829847)
XLA Ops:
  0.6 15.4 %moments.1 = (f32[16,224,128]{2,1,0:T(8,128)S(1)}, f32[16,224,128]{2,1,0:T(8,128)S(1)}) custom-call(s32[1]{0:T(128)} %bitcast.place, s32[8,19]{1,0:T(8,128)} %bitcast.19, s32[19]{0:T(128)} %bitcast.21, f32[5,19]{1,0:T(8,128)} %bitcast.20, bf16[32,128,128]{2,1,0:T(8,128)(2,1)} %bitcast.18, bf16[19,5,128,128]{3,2,1,0:T(8,128)(2,1)} %fac_any.1, ...), custom_call_target="tpu_custom_call" | custom-call | tf_op jit(solution)/shard_map/moments/pallas_call | solution.py:222
  16.0 4.3 %collective-permute-start = (f32[16,224,128]{2,1,0:T(8,128)S(1)}, f32[16,224,128]{2,1,0:T(8,128)S(1)}, u32[]{:S(2)}, u32[]{:S(2)}) collective-permute-start(f32[16,224,128]{2,1,0:T(8,128)S(1)} %get-tuple-element.12), channel_id=1, source_target_pairs={{0,1},{1,0},{2,3},{3,2},{4,5},{5,4},{6,7},{7,6},{8,9},{9,8},{10,11... | collective-permute-start | bytes 5505032 | tf_op jit(solution)/shard_map/ppermute | solution.py:453
  20.3 3.4 %collective-permute-done = f32[16,224,128]{2,1,0:T(8,128)S(1)} collective-permute-done((f32[16,224,128]{2,1,0:T(8,128)S(1)}, f32[16,224,128]{2,1,0:T(8,128)S(1)}, u32[]{:S(2)}, u32[]{:S(2)}) %collective-permute-start) | collective-permute-done | bytes 1835040 | tf_op jit(solution)/shard_map/ppermute | solution.py:453
  23.7 0.3 add.20
  24.0 32.4 %all_to_all.10 = f32[32,112,128]{2,1,0:T(8,128)S(1)} all-to-all(f32[32,112,128]{2,1,0:T(8,128)S(1)} %bitcast.16), channel_id=1, replica_groups=mesh['x'=4,'far'=4,'near'=2,'y'=4,'core'=2] {'x','y','near'}, dimensions={0} | all-to-all | bytes 3670016 | tf_op jit(solution)/shard_map/all_to_all | solution.py:476
  56.4 0.0 copy-start
  56.4 0.1 reduce_sum.9
  56.5 4.7 %collective-permute-start.3 = (f32[112,128]{1,0:T(8,128)S(1)}, f32[112,128]{1,0:T(8,128)S(1)}, u32[]{:S(2)}, u32[]{:S(2)}) collective-permute-start(f32[112,128]{1,0:T(8,128)S(1)} %reduce_sum.9), channel_id=1, source_target_pairs={{0,48},{16,0},{32,16},{48,32},{1,49},{17,1},{33,17},{49,33},{2,50}... | collective-permute-start | bytes 172040 | tf_op jit(solution)/shard_map/ppermute | solution.py:459
  61.2 0.0 collective-permute-start.2
  61.3 4.2 %collective-permute-start.1 = (f32[112,128]{1,0:T(8,128)S(1)}, f32[112,128]{1,0:T(8,128)S(1)}, u32[]{:S(2)}, u32[]{:S(2)}) collective-permute-start(f32[112,128]{1,0:T(8,128)S(1)} %reduce_sum.9), channel_id=1, source_target_pairs={{0,32},{16,48},{32,0},{48,16},{1,33},{17,49},{33,1},{49,17},{2,34}... | collective-permute-start | bytes 172040 | tf_op jit(solution)/shard_map/ppermute | solution.py:459
  65.4 0.0 collective-permute-done.3
  65.4 1.3 %collective-permute-done.2 = f32[112,128]{1,0:T(8,128)S(1)} collective-permute-done((f32[112,128]{1,0:T(8,128)S(1)}, f32[112,128]{1,0:T(8,128)S(1)}, u32[]{:S(2)}, u32[]{:S(2)}) %collective-permute-start.2) | collective-permute-done | bytes 57376 | tf_op jit(solution)/shard_map/ppermute | solution.py:459
  66.7 1.7 %collective-permute-done.1 = f32[112,128]{1,0:T(8,128)S(1)} collective-permute-done((f32[112,128]{1,0:T(8,128)S(1)}, f32[112,128]{1,0:T(8,128)S(1)}, u32[]{:S(2)}, u32[]{:S(2)}) %collective-permute-start.1) | collective-permute-done | bytes 57376 | tf_op jit(solution)/shard_map/ppermute | solution.py:459
  68.4 0.2 collective-permute-start.4
  68.6 0.1 pad_add_fusion.place
  68.7 3.3 %collective-permute-done.4.theirs_ref = f32[112,128]{1,0:T(8,128)S(1)} collective-permute-done((f32[112,128]{1,0:T(8,128)S(1)}, f32[112,128]{1,0:T(8,128)S(1)}, u32[]{:S(2)}, u32[]{:S(2)}) %collective-permute-start.4) | collective-permute-done | bytes 57376 | tf_op jit(solution)/shard_map/ppermute | solution.py:479
  72.0 0.0 copy-done
  72.0 6.1 %solve.1 = f32[216,128]{1,0:T(8,128)S(1)} custom-call(s32[2]{0:T(128)S(1)} %pad_add_fusion.place, f32[112,128]{1,0:T(8,128)S(1)} %add_add_fusion.mine_ref, f32[112,128]{1,0:T(8,128)S(1)} %collective-permute-done.4.theirs_ref, f32[5,19,128]{2,1,0:T(8,128)S(1)} %bitcast.15), custom_call_target="tpu_custom_call" | custom-call | tf_op jit(solution)/shard_map/solve/pallas_call | solution.py:345
  78.1 0.1 broadcast_in_dim.10
  78.3 22.4 %all_to_all.11.part_ref = f32[16,216,128]{2,1,0:T(8,128)S(1)} all-to-all(f32[16,216,128]{2,1,0:T(8,128)S(1)} %broadcast_in_dim.10), channel_id=1, replica_groups=mesh['x'=4,'far'=4,'near'=2,'y'=4,'core'=2] {'x','y'}, dimensions={0} | all-to-all | bytes 3538944 | tf_op jit(solution)/shard_map/all_to_all | solution.py:484
  100.7 5.8 %collective-permute-start.5 = (f32[16,216,128]{2,1,0:T(8,128)S(1)}, f32[16,216,128]{2,1,0:T(8,128)S(1)}, u32[]{:S(2)}, u32[]{:S(2)}) collective-permute-start(f32[16,216,128]{2,1,0:T(8,128)S(1)} %all_to_all.11.part_ref), channel_id=1, source_target_pairs={{0,1},{1,0},{2,3},{3,2},{4,5},{5,4},{6,7},{7,6},{8,9},{9,8},{10,11... | collective-permute-start | bytes 5308424 | tf_op jit(solution)/shard_map/ppermute | solution.py:453
  106.5 2.6 %unpack_first.1 = (f32[95,128,128]{2,1,0:T(8,128)}, f32[5,24,128]{2,1,0:T(8,128)S(1)}, f32[5,24,128]{2,1,0:T(8,128)S(1)}) custom-call(s32[1]{0:T(128)} %bitcast.place, f32[16,216,128]{2,1,0:T(8,128)S(1)} %all_to_all.11.part_ref), custom_call_target="tpu_custom_call" | custom-call | flops 4000000 | bytes 5000000 | tf_op jit(solution)/shard_map/unpack_first/pallas_call | solution.py:425
  109.1 0.7 collective-permute-done.5.part_ref
  109.8 3.3 %unpack_last.1 = (f32[95,128,128]{2,1,0:T(8,128)}, f32[5,19,128]{2,1,0:T(8,128)}, f32[5,19]{1,0:T(8,128)}) custom-call(s32[1]{0:T(128)} %bitcast.place, f32[16,216,128]{2,1,0:T(8,128)S(1)} %collective-permute-done.5.part_ref, f32[95,128,128]{2,1,0:T(8,128)} %get-tuple-element.13.begun_any, ...), custom_call_target="tpu_custom_call", output_to_operand_aliasing={{0}: (2, {})} | custom-call | flops 4000000 | bytes 5000000 | tf_op jit(solution)/shard_map/unpack_last/pallas_call | solution.py:435
  (1 shorter events, 0.0 us)
Async XLA Ops:
  16.0 7.7 %collective-permute-start = (f32[16,224,128]{2,1,0:T(8,128)S(1)}, f32[16,224,128]{2,1,0:T(8,128)S(1)}, u32[]{:S(2)}, u32[]{:S(2)}) collective-permute-start(f32[16,224,128]{2,1,0:T(8,128)S(1)} %get-tuple-element.12), channel_id=1, source_target_pairs={{0,1},{1,0},{2,3},{3,2},{4,5},{5,4},{6,7},{7,6},{8,9},{9,8},{10,11... | collective-permute-start | bytes 5505032 | tf_op jit(solution)/shard_map/ppermute | solution.py:453
  56.4 15.6 %copy-start = (f32[19,5,128]{2,0,1:T(8,128)S(1)}, f32[19,5,128]{2,0,1:T(8,128)}, u32[]{:S(2)}) copy-start(f32[19,5,128]{2,0,1:T(8,128)} %param.9) | copy-start | bytes 145924
  56.5 8.9 %collective-permute-start.3 = (f32[112,128]{1,0:T(8,128)S(1)}, f32[112,128]{1,0:T(8,128)S(1)}, u32[]{:S(2)}, u32[]{:S(2)}) collective-permute-start(f32[112,128]{1,0:T(8,128)S(1)} %reduce_sum.9), channel_id=1, source_target_pairs={{0,48},{16,0},{32,16},{48,32},{1,49},{17,1},{33,17},{49,33},{2,50}... | collective-permute-start | bytes 172040 | tf_op jit(solution)/shard_map/ppermute | solution.py:459
  61.2 5.4 %collective-permute-start.2 = (f32[112,128]{1,0:T(8,128)S(1)}, f32[112,128]{1,0:T(8,128)S(1)}, u32[]{:S(2)}, u32[]{:S(2)}) collective-permute-start(f32[112,128]{1,0:T(8,128)S(1)} %reduce_sum.9), channel_id=1, source_target_pairs={{0,16},{16,32},{32,48},{48,0},{1,17},{17,33},{33,49},{49,1},{2,18}... | collective-permute-start | bytes 172040 | tf_op jit(solution)/shard_map/ppermute | solution.py:459
  61.3 7.1 %collective-permute-start.1 = (f32[112,128]{1,0:T(8,128)S(1)}, f32[112,128]{1,0:T(8,128)S(1)}, u32[]{:S(2)}, u32[]{:S(2)}) collective-permute-start(f32[112,128]{1,0:T(8,128)S(1)} %reduce_sum.9), channel_id=1, source_target_pairs={{0,32},{16,48},{32,0},{48,16},{1,33},{17,49},{33,1},{49,17},{2,34}... | collective-permute-start | bytes 172040 | tf_op jit(solution)/shard_map/ppermute | solution.py:459
  68.4 3.7 %collective-permute-start.4 = (f32[112,128]{1,0:T(8,128)S(1)}, f32[112,128]{1,0:T(8,128)S(1)}, u32[]{:S(2)}, u32[]{:S(2)}) collective-permute-start(f32[112,128]{1,0:T(8,128)S(1)} %add_add_fusion.mine_ref), channel_id=1, source_target_pairs={{0,8},{8,0},{1,9},{9,1},{2,10},{10,2},{3,11},{11,3},{4,12},{12,4},... | collective-permute-start | bytes 172040 | tf_op jit(solution)/shard_map/ppermute | solution.py:479
  100.7 9.1 %collective-permute-start.5 = (f32[16,216,128]{2,1,0:T(8,128)S(1)}, f32[16,216,128]{2,1,0:T(8,128)S(1)}, u32[]{:S(2)}, u32[]{:S(2)}) collective-permute-start(f32[16,216,128]{2,1,0:T(8,128)S(1)} %all_to_all.11.part_ref), channel_id=1, source_target_pairs={{0,1},{1,0},{2,3},{3,2},{4,5},{5,4},{6,7},{7,6},{8,9},{9,8},{10,11... | collective-permute-start | bytes 5308424 | tf_op jit(solution)/shard_map/ppermute | solution.py:453

commit v5 on v4

--- a/solution.py
+++ b/solution.py
@@ -16,7 +16,7 @@
 BF16 = jnp.bfloat16
 SLOTS = 9
 GROUP = 3
-UNROLL = 2
+UNROLL = 3
 OWNERS = 16
 HALF = GROUP * OWNERS
 SHARE = 224
@@ -88,8 +88,6 @@
     acc[...] = jnp.zeros_like(acc)
     tot[...] = jnp.zeros_like(tot)
     cnt[...] = jnp.zeros_like(cnt)
-    gate[...] = jnp.zeros_like(gate)
-    rows_t[...] = jnp.zeros_like(rows_t)
 
     copies[0].wait()
     copies[1].wait()
@@ -184,16 +182,24 @@
         shift[u] = jnp.concatenate(lines + [jnp.zeros((WIDTH - 3 * COMPS, WIDTH), F32)], axis=0).T
         const[u] = jnp.sum(jnp.log(diag), axis=1, keepdims=True) + prior
 
+    def stage(work, j):
+        for u in range(UNROLL):
+            work(UNROLL * j + u, u)
+
     def step(j, carry):
-        for u in range(UNROLL):
-            moments_of(UNROLL * (j - 2) + u, u)
-        for u in range(UNROLL):
-            scores_of(UNROLL * (j - 1) + u, u)
-        for u in range(UNROLL):
-            prepare(UNROLL * j + u, u)
+        stage(moments_of, j - 2)
+        stage(scores_of, j - 1)
+        stage(prepare, j)
         return carry
 
-    lax.fori_loop(0, (total_items + UNROLL - 1) // UNROLL + 2, step, 0)
+    groups = (total_items + UNROLL - 1) // UNROLL
+    stage(prepare, 0)
+    stage(scores_of, 0)
+    stage(prepare, 1)
+    lax.fori_loop(2, groups, step, 0)
+    stage(moments_of, jnp.maximum(groups - 2, 0))
+    stage(scores_of, groups - 1)
+    stage(moments_of, groups - 1)
 
     def pack(q, carry):
         for base, out_ref in ((place[0], own_ref), (1 - place[0], other_ref)):

time: 113 us -> 110 us (0.973)
  Pallas kernels: 27.4 us -> 22.3 us
  starting transfers between devices: 19.2 us -> 21.4 us
    pallas_call x1, Pallas kernels: 15.4 us -> 10.3 us  [local_moments(): pl.pallas_call(moments_kernel, in_specs=[smem] + [anywhere] * 6, out_spec...]
    ppermute x2, starting transfers between devices: 10 us -> 14.2 us  [swap_cores(): return lax.ppermute(value, 'core', [(0, 1), (1, 0)])]
    ppermute x3, starting transfers between devices: 8.89 us -> 6.71 us  [sum_far(): lax.ppermute(value, 'far', [(i, (i + hop) % 4) for i in range(4)])]
where the time goes in v5:
time: 110 us
  blocking collectives  54.3 us (49%)
  Pallas kernels  22.3 us (20%)
  starting transfers between devices  21.4 us (19%)
  waiting for transfers between devices  10.6 us (10%)
    all_to_all x1, blocking collectives, body(): lax.all_to_all(half.reshape(2 * OWNERS, PART, width), peers, 0, 0, tiled=...  31.8 us
    all_to_all x1, blocking collectives, body(): here = lax.all_to_all(spread, ('x', 'y'), 0, 0, tiled=True)  22.5 us
    ppermute x2, starting transfers between devices, swap_cores(): return lax.ppermute(value, 'core', [(0, 1), (1, 0)])  14.2 us
    pallas_call x1, Pallas kernels, local_moments(): pl.pallas_call(moments_kernel, in_specs=[smem] + [anywhere] * 6, out_spec...  10.3 us
    ppermute x3, starting transfers between devices, sum_far(): lax.ppermute(value, 'far', [(i, (i + hop) % 4) for i in range(4)])  6.71 us
    pallas_call x1, Pallas kernels, solve_share(): pl.pallas_call(solve_kernel, in_specs=[smem, vmem, vmem, vmem], out_specs...  6.08 us
    ppermute x2, waiting for transfers between devices, swap_cores(): return lax.ppermute(value, 'core', [(0, 1), (1, 0)])  4.09 us
    ppermute x3, waiting for transfers between devices, sum_far(): lax.ppermute(value, 'far', [(i, (i + hop) % 4) for i in range(4)])  3.36 us
  transfers between devices with their start and end apart: 6, of which 5 were waited for; matrix products, arithmetic and copies ran while one was open for 0% of the time, Pallas kernels for 2%

profile of v5, /device:TPU:1, one launch (start us, length us, event | category | flops | bytes accessed | tf_op | source)
XLA Modules:
  0.0 110.0 jit_solution(10711200762434272012)
XLA Ops:
  0.6 10.3 %moments.1 = (f32[16,224,128]{2,1,0:T(8,128)S(1)}, f32[16,224,128]{2,1,0:T(8,128)S(1)}) custom-call(s32[1]{0:T(128)} %bitcast.place, s32[8,19]{1,0:T(8,128)} %bitcast.19, s32[19]{0:T(128)} %bitcast.21, f32[5,19]{1,0:T(8,128)} %bitcast.20, bf16[32,128,128]{2,1,0:T(8,128)(2,1)} %bitcast.18, bf16[19,5,128,128]{3,2,1,0:T(8,128)(2,1)} %fac_any.1, ...), custom_call_target="tpu_custom_call" | custom-call | tf_op jit(solution)/shard_map/moments/pallas_call | solution.py:228
  11.0 8.5 %collective-permute-start = (f32[16,224,128]{2,1,0:T(8,128)S(1)}, f32[16,224,128]{2,1,0:T(8,128)S(1)}, u32[]{:S(2)}, u32[]{:S(2)}) collective-permute-start(f32[16,224,128]{2,1,0:T(8,128)S(1)} %get-tuple-element.12), channel_id=1, source_target_pairs={{0,1},{1,0},{2,3},{3,2},{4,5},{5,4},{6,7},{7,6},{8,9},{9,8},{10,11... | collective-permute-start | bytes 5505032 | tf_op jit(solution)/shard_map/ppermute | solution.py:459
  19.5 3.4 %collective-permute-done = f32[16,224,128]{2,1,0:T(8,128)S(1)} collective-permute-done((f32[16,224,128]{2,1,0:T(8,128)S(1)}, f32[16,224,128]{2,1,0:T(8,128)S(1)}, u32[]{:S(2)}, u32[]{:S(2)}) %collective-permute-start) | collective-permute-done | bytes 1835040 | tf_op jit(solution)/shard_map/ppermute | solution.py:459
  22.9 0.3 add.20
  23.2 31.8 %all_to_all.10 = f32[32,112,128]{2,1,0:T(8,128)S(1)} all-to-all(f32[32,112,128]{2,1,0:T(8,128)S(1)} %bitcast.16), channel_id=1, replica_groups=mesh['x'=4,'far'=4,'near'=2,'y'=4,'core'=2] {'x','y','near'}, dimensions={0} | all-to-all | bytes 3670016 | tf_op jit(solution)/shard_map/all_to_all | solution.py:482
  55.0 0.0 copy-start
  55.0 0.1 reduce_sum.9
  55.1 2.8 %collective-permute-start.3 = (f32[112,128]{1,0:T(8,128)S(1)}, f32[112,128]{1,0:T(8,128)S(1)}, u32[]{:S(2)}, u32[]{:S(2)}) collective-permute-start(f32[112,128]{1,0:T(8,128)S(1)} %reduce_sum.9), channel_id=1, source_target_pairs={{0,48},{16,0},{32,16},{48,32},{1,49},{17,1},{33,17},{49,33},{2,50}... | collective-permute-start | bytes 172040 | tf_op jit(solution)/shard_map/ppermute | solution.py:465
  57.9 0.0 collective-permute-start.2
  57.9 3.9 %collective-permute-start.1 = (f32[112,128]{1,0:T(8,128)S(1)}, f32[112,128]{1,0:T(8,128)S(1)}, u32[]{:S(2)}, u32[]{:S(2)}) collective-permute-start(f32[112,128]{1,0:T(8,128)S(1)} %reduce_sum.9), channel_id=1, source_target_pairs={{0,32},{16,48},{32,0},{48,16},{1,33},{17,49},{33,1},{49,17},{2,34}... | collective-permute-start | bytes 172040 | tf_op jit(solution)/shard_map/ppermute | solution.py:465
  61.8 0.0 collective-permute-done.3
  61.8 1.5 %collective-permute-done.2 = f32[112,128]{1,0:T(8,128)S(1)} collective-permute-done((f32[112,128]{1,0:T(8,128)S(1)}, f32[112,128]{1,0:T(8,128)S(1)}, u32[]{:S(2)}, u32[]{:S(2)}) %collective-permute-start.2) | collective-permute-done | bytes 57376 | tf_op jit(solution)/shard_map/ppermute | solution.py:465
  63.2 1.9 %collective-permute-done.1 = f32[112,128]{1,0:T(8,128)S(1)} collective-permute-done((f32[112,128]{1,0:T(8,128)S(1)}, f32[112,128]{1,0:T(8,128)S(1)}, u32[]{:S(2)}, u32[]{:S(2)}) %collective-permute-start.1) | collective-permute-done | bytes 57376 | tf_op jit(solution)/shard_map/ppermute | solution.py:465
  65.1 0.5 collective-permute-start.4
  65.6 0.1 pad_add_fusion.place
  65.7 3.2 %collective-permute-done.4.theirs_ref = f32[112,128]{1,0:T(8,128)S(1)} collective-permute-done((f32[112,128]{1,0:T(8,128)S(1)}, f32[112,128]{1,0:T(8,128)S(1)}, u32[]{:S(2)}, u32[]{:S(2)}) %collective-permute-start.4) | collective-permute-done | bytes 57376 | tf_op jit(solution)/shard_map/ppermute | solution.py:485
  68.8 0.0 copy-done
  68.8 6.1 %solve.1 = f32[216,128]{1,0:T(8,128)S(1)} custom-call(s32[2]{0:T(128)S(1)} %pad_add_fusion.place, f32[112,128]{1,0:T(8,128)S(1)} %add_add_fusion.mine_ref, f32[112,128]{1,0:T(8,128)S(1)} %collective-permute-done.4.theirs_ref, f32[5,19,128]{2,1,0:T(8,128)S(1)} %bitcast.15), custom_call_target="tpu_custom_call" | custom-call | tf_op jit(solution)/shard_map/solve/pallas_call | solution.py:351
  74.9 0.1 broadcast_in_dim.10
  75.0 22.5 %all_to_all.11.part_ref = f32[16,216,128]{2,1,0:T(8,128)S(1)} all-to-all(f32[16,216,128]{2,1,0:T(8,128)S(1)} %broadcast_in_dim.10), channel_id=1, replica_groups=mesh['x'=4,'far'=4,'near'=2,'y'=4,'core'=2] {'x','y'}, dimensions={0} | all-to-all | bytes 3538944 | tf_op jit(solution)/shard_map/all_to_all | solution.py:490
  97.6 5.7 %collective-permute-start.5 = (f32[16,216,128]{2,1,0:T(8,128)S(1)}, f32[16,216,128]{2,1,0:T(8,128)S(1)}, u32[]{:S(2)}, u32[]{:S(2)}) collective-permute-start(f32[16,216,128]{2,1,0:T(8,128)S(1)} %all_to_all.11.part_ref), channel_id=1, source_target_pairs={{0,1},{1,0},{2,3},{3,2},{4,5},{5,4},{6,7},{7,6},{8,9},{9,8},{10,11... | collective-permute-start | bytes 5308424 | tf_op jit(solution)/shard_map/ppermute | solution.py:459
  103.3 2.6 %unpack_first.1 = (f32[95,128,128]{2,1,0:T(8,128)}, f32[5,24,128]{2,1,0:T(8,128)S(1)}, f32[5,24,128]{2,1,0:T(8,128)S(1)}) custom-call(s32[1]{0:T(128)} %bitcast.place, f32[16,216,128]{2,1,0:T(8,128)S(1)} %all_to_all.11.part_ref), custom_call_target="tpu_custom_call" | custom-call | flops 4000000 | bytes 5000000 | tf_op jit(solution)/shard_map/unpack_first/pallas_call | solution.py:431
  105.9 0.7 collective-permute-done.5.part_ref
  106.6 3.3 %unpack_last.1 = (f32[95,128,128]{2,1,0:T(8,128)}, f32[5,19,128]{2,1,0:T(8,128)}, f32[5,19]{1,0:T(8,128)}) custom-call(s32[1]{0:T(128)} %bitcast.place, f32[16,216,128]{2,1,0:T(8,128)S(1)} %collective-permute-done.5.part_ref, f32[95,128,128]{2,1,0:T(8,128)} %get-tuple-element.13.begun_any, ...), custom_call_target="tpu_custom_call", output_to_operand_aliasing={{0}: (2, {})} | custom-call | flops 4000000 | bytes 5000000 | tf_op jit(solution)/shard_map/unpack_last/pallas_call | solution.py:441
  (1 shorter events, 0.0 us)
Async XLA Ops:
  11.0 11.9 %collective-permute-start = (f32[16,224,128]{2,1,0:T(8,128)S(1)}, f32[16,224,128]{2,1,0:T(8,128)S(1)}, u32[]{:S(2)}, u32[]{:S(2)}) collective-permute-start(f32[16,224,128]{2,1,0:T(8,128)S(1)} %get-tuple-element.12), channel_id=1, source_target_pairs={{0,1},{1,0},{2,3},{3,2},{4,5},{5,4},{6,7},{7,6},{8,9},{9,8},{10,11... | collective-permute-start | bytes 5505032 | tf_op jit(solution)/shard_map/ppermute | solution.py:459
  55.0 13.9 %copy-start = (f32[19,5,128]{2,0,1:T(8,128)S(1)}, f32[19,5,128]{2,0,1:T(8,128)}, u32[]{:S(2)}) copy-start(f32[19,5,128]{2,0,1:T(8,128)} %param.9) | copy-start | bytes 145924
  55.1 6.7 %collective-permute-start.3 = (f32[112,128]{1,0:T(8,128)S(1)}, f32[112,128]{1,0:T(8,128)S(1)}, u32[]{:S(2)}, u32[]{:S(2)}) collective-permute-start(f32[112,128]{1,0:T(8,128)S(1)} %reduce_sum.9), channel_id=1, source_target_pairs={{0,48},{16,0},{32,16},{48,32},{1,49},{17,1},{33,17},{49,33},{2,50}... | collective-permute-start | bytes 172040 | tf_op jit(solution)/shard_map/ppermute | solution.py:465
  57.9 5.4 %collective-permute-start.2 = (f32[112,128]{1,0:T(8,128)S(1)}, f32[112,128]{1,0:T(8,128)S(1)}, u32[]{:S(2)}, u32[]{:S(2)}) collective-permute-start(f32[112,128]{1,0:T(8,128)S(1)} %reduce_sum.9), channel_id=1, source_target_pairs={{0,16},{16,32},{32,48},{48,0},{1,17},{17,33},{33,49},{49,1},{2,18}... | collective-permute-start | bytes 172040 | tf_op jit(solution)/shard_map/ppermute | solution.py:465
  57.9 7.3 %collective-permute-start.1 = (f32[112,128]{1,0:T(8,128)S(1)}, f32[112,128]{1,0:T(8,128)S(1)}, u32[]{:S(2)}, u32[]{:S(2)}) collective-permute-start(f32[112,128]{1,0:T(8,128)S(1)} %reduce_sum.9), channel_id=1, source_target_pairs={{0,32},{16,48},{32,0},{48,16},{1,33},{17,49},{33,1},{49,17},{2,34}... | collective-permute-start | bytes 172040 | tf_op jit(solution)/shard_map/ppermute | solution.py:465
  65.1 3.7 %collective-permute-start.4 = (f32[112,128]{1,0:T(8,128)S(1)}, f32[112,128]{1,0:T(8,128)S(1)}, u32[]{:S(2)}, u32[]{:S(2)}) collective-permute-start(f32[112,128]{1,0:T(8,128)S(1)} %add_add_fusion.mine_ref), channel_id=1, source_target_pairs={{0,8},{8,0},{1,9},{9,1},{2,10},{10,2},{3,11},{11,3},{4,12},{12,4},... | collective-permute-start | bytes 172040 | tf_op jit(solution)/shard_map/ppermute | solution.py:485
  97.6 9.1 %collective-permute-start.5 = (f32[16,216,128]{2,1,0:T(8,128)S(1)}, f32[16,216,128]{2,1,0:T(8,128)S(1)}, u32[]{:S(2)}, u32[]{:S(2)}) collective-permute-start(f32[16,216,128]{2,1,0:T(8,128)S(1)} %all_to_all.11.part_ref), channel_id=1, source_target_pairs={{0,1},{1,0},{2,3},{3,2},{4,5},{5,4},{6,7},{7,6},{8,9},{9,8},{10,11... | collective-permute-start | bytes 5308424 | tf_op jit(solution)/shard_map/ppermute | solution.py:459

commit v6 on v5

--- a/solution.py
+++ b/solution.py
@@ -361,7 +361,8 @@
 def unpack_half(half, part_ref, factor_any, mean_ref, counts, buffer, sems):
     def copy_of(at):
         comp = half * HALF + at
-        copy = pltpu.make_async_copy(buffer.at[at], factor_any.at[comp], sems.at[at])
+        target = factor_any.at[jnp.minimum(comp, CLASSES * COMPS - 1)]
+        copy = pltpu.make_async_copy(buffer.at[at], target, sems.at[at])
         return comp < CLASSES * COMPS, copy
 
     def unpack(q, carry):

time: 110 us -> 112 us (1.018)
  starting transfers between devices: 21.4 us -> 23.3 us
  blocking collectives: 54.3 us -> 52.5 us
    ppermute x3, starting transfers between devices: 6.71 us -> 9.47 us  [sum_far(): lax.ppermute(value, 'far', [(i, (i + hop) % 4) for i in range(4)])]
    all_to_all x1, blocking collectives: 31.8 us -> 29.3 us  [body(): lax.all_to_all(half.reshape(2 * OWNERS, PART, width), peers, 0, 0, tiled=...]
    ppermute x3, waiting for transfers between devices: 3.36 us -> 4.51 us  [sum_far(): lax.ppermute(value, 'far', [(i, (i + hop) % 4) for i in range(4)])]
where the time goes in v6:
time: 112 us; the launch traced here: 111 us
  blocking collectives  52.5 us (47%)
  starting transfers between devices  23.3 us (21%)
  Pallas kernels  22.3 us (20%)
  waiting for transfers between devices  11.5 us (10%)
    all_to_all x1, blocking collectives, body(): lax.all_to_all(half.reshape(2 * OWNERS, PART, width), peers, 0, 0, tiled=...  29.3 us
    all_to_all x1, blocking collectives, body(): here = lax.all_to_all(spread, ('x', 'y'), 0, 0, tiled=True)  23.2 us
    ppermute x2, starting transfers between devices, swap_cores(): return lax.ppermute(value, 'core', [(0, 1), (1, 0)])  13.6 us
    pallas_call x1, Pallas kernels, local_moments(): pl.pallas_call(moments_kernel, in_specs=[smem] + [anywhere] * 6, out_spec...  10.3 us
    ppermute x3, starting transfers between devices, sum_far(): lax.ppermute(value, 'far', [(i, (i + hop) % 4) for i in range(4)])  9.47 us
    pallas_call x1, Pallas kernels, solve_share(): pl.pallas_call(solve_kernel, in_specs=[smem, vmem, vmem, vmem], out_specs...  6.08 us
    ppermute x3, waiting for transfers between devices, sum_far(): lax.ppermute(value, 'far', [(i, (i + hop) % 4) for i in range(4)])  4.51 us
    ppermute x2, waiting for transfers between devices, swap_cores(): return lax.ppermute(value, 'core', [(0, 1), (1, 0)])  4.09 us
  transfers between devices with their start and end apart: 6, of which 5 were waited for; matrix products, arithmetic and copies ran while one was open for 0% of the time, Pallas kernels for 2%

profile of v6, /device:TPU:1, one launch (start us, length us, event | category | flops | bytes accessed | tf_op | source)
XLA Modules:
  0.0 111.1 jit_solution(15573641819757528157)
XLA Ops:
  0.6 10.3 %moments.1 = (f32[16,224,128]{2,1,0:T(8,128)S(1)}, f32[16,224,128]{2,1,0:T(8,128)S(1)}) custom-call(s32[1]{0:T(128)} %bitcast.place, s32[8,19]{1,0:T(8,128)} %bitcast.19, s32[19]{0:T(128)} %bitcast.21, f32[5,19]{1,0:T(8,128)} %bitcast.20, bf16[32,128,128]{2,1,0:T(8,128)(2,1)} %bitcast.18, bf16[19,5,128,128]{3,2,1,0:T(8,128)(2,1)} %fac_any.1, ...), custom_call_target="tpu_custom_call" | custom-call | tf_op jit(solution)/shard_map/moments/pallas_call | solution.py:228
  11.0 8.5 %collective-permute-start = (f32[16,224,128]{2,1,0:T(8,128)S(1)}, f32[16,224,128]{2,1,0:T(8,128)S(1)}, u32[]{:S(2)}, u32[]{:S(2)}) collective-permute-start(f32[16,224,128]{2,1,0:T(8,128)S(1)} %get-tuple-element.12), channel_id=1, source_target_pairs={{0,1},{1,0},{2,3},{3,2},{4,5},{5,4},{6,7},{7,6},{8,9},{9,8},{10,11... | collective-permute-start | bytes 5505032 | tf_op jit(solution)/shard_map/ppermute | solution.py:460
  19.5 3.4 %collective-permute-done = f32[16,224,128]{2,1,0:T(8,128)S(1)} collective-permute-done((f32[16,224,128]{2,1,0:T(8,128)S(1)}, f32[16,224,128]{2,1,0:T(8,128)S(1)}, u32[]{:S(2)}, u32[]{:S(2)}) %collective-permute-start) | collective-permute-done | bytes 1835040 | tf_op jit(solution)/shard_map/ppermute | solution.py:460
  22.9 0.3 add.20
  23.2 29.3 %all_to_all.10 = f32[32,112,128]{2,1,0:T(8,128)S(1)} all-to-all(f32[32,112,128]{2,1,0:T(8,128)S(1)} %bitcast.16), channel_id=1, replica_groups=mesh['x'=4,'far'=4,'near'=2,'y'=4,'core'=2] {'x','y','near'}, dimensions={0} | all-to-all | bytes 3670016 | tf_op jit(solution)/shard_map/all_to_all | solution.py:483
  52.5 0.0 copy-start
  52.5 0.1 reduce_sum.9
  52.6 6.1 %collective-permute-start.3 = (f32[112,128]{1,0:T(8,128)S(1)}, f32[112,128]{1,0:T(8,128)S(1)}, u32[]{:S(2)}, u32[]{:S(2)}) collective-permute-start(f32[112,128]{1,0:T(8,128)S(1)} %reduce_sum.9), channel_id=1, source_target_pairs={{0,48},{16,0},{32,16},{48,32},{1,49},{17,1},{33,17},{49,33},{2,50}... | collective-permute-start | bytes 172040 | tf_op jit(solution)/shard_map/ppermute | solution.py:466
  58.7 0.0 collective-permute-start.2
  58.7 3.4 %collective-permute-start.1 = (f32[112,128]{1,0:T(8,128)S(1)}, f32[112,128]{1,0:T(8,128)S(1)}, u32[]{:S(2)}, u32[]{:S(2)}) collective-permute-start(f32[112,128]{1,0:T(8,128)S(1)} %reduce_sum.9), channel_id=1, source_target_pairs={{0,32},{16,48},{32,0},{48,16},{1,33},{17,49},{33,1},{49,17},{2,34}... | collective-permute-start | bytes 172040 | tf_op jit(solution)/shard_map/ppermute | solution.py:466
  62.1 0.0 collective-permute-done.3
  62.1 1.8 %collective-permute-done.2 = f32[112,128]{1,0:T(8,128)S(1)} collective-permute-done((f32[112,128]{1,0:T(8,128)S(1)}, f32[112,128]{1,0:T(8,128)S(1)}, u32[]{:S(2)}, u32[]{:S(2)}) %collective-permute-start.2) | collective-permute-done | bytes 57376 | tf_op jit(solution)/shard_map/ppermute | solution.py:466
  63.8 2.8 %collective-permute-done.1 = f32[112,128]{1,0:T(8,128)S(1)} collective-permute-done((f32[112,128]{1,0:T(8,128)S(1)}, f32[112,128]{1,0:T(8,128)S(1)}, u32[]{:S(2)}, u32[]{:S(2)}) %collective-permute-start.1) | collective-permute-done | bytes 57376 | tf_op jit(solution)/shard_map/ppermute | solution.py:466
  66.6 0.3 collective-permute-start.4
  66.9 0.1 pad_add_fusion.place
  67.0 2.9 %collective-permute-done.4.theirs_ref = f32[112,128]{1,0:T(8,128)S(1)} collective-permute-done((f32[112,128]{1,0:T(8,128)S(1)}, f32[112,128]{1,0:T(8,128)S(1)}, u32[]{:S(2)}, u32[]{:S(2)}) %collective-permute-start.4) | collective-permute-done | bytes 57376 | tf_op jit(solution)/shard_map/ppermute | solution.py:486
  69.9 0.0 copy-done
  69.9 6.1 %solve.1 = f32[216,128]{1,0:T(8,128)S(1)} custom-call(s32[2]{0:T(128)S(1)} %pad_add_fusion.place, f32[112,128]{1,0:T(8,128)S(1)} %add_add_fusion.mine_ref, f32[112,128]{1,0:T(8,128)S(1)} %collective-permute-done.4.theirs_ref, f32[5,19,128]{2,1,0:T(8,128)S(1)} %bitcast.15), custom_call_target="tpu_custom_call" | custom-call | tf_op jit(solution)/shard_map/solve/pallas_call | solution.py:351
  76.0 0.1 broadcast_in_dim.10
  76.1 23.2 %all_to_all.11.part_ref = f32[16,216,128]{2,1,0:T(8,128)S(1)} all-to-all(f32[16,216,128]{2,1,0:T(8,128)S(1)} %broadcast_in_dim.10), channel_id=1, replica_groups=mesh['x'=4,'far'=4,'near'=2,'y'=4,'core'=2] {'x','y'}, dimensions={0} | all-to-all | bytes 3538944 | tf_op jit(solution)/shard_map/all_to_all | solution.py:491
  99.3 5.0 %collective-permute-start.5 = (f32[16,216,128]{2,1,0:T(8,128)S(1)}, f32[16,216,128]{2,1,0:T(8,128)S(1)}, u32[]{:S(2)}, u32[]{:S(2)}) collective-permute-start(f32[16,216,128]{2,1,0:T(8,128)S(1)} %all_to_all.11.part_ref), channel_id=1, source_target_pairs={{0,1},{1,0},{2,3},{3,2},{4,5},{5,4},{6,7},{7,6},{8,9},{9,8},{10,11... | collective-permute-start | bytes 5308424 | tf_op jit(solution)/shard_map/ppermute | solution.py:460
  104.3 2.6 %unpack_first.1 = (f32[95,128,128]{2,1,0:T(8,128)}, f32[5,24,128]{2,1,0:T(8,128)S(1)}, f32[5,24,128]{2,1,0:T(8,128)S(1)}) custom-call(s32[1]{0:T(128)} %bitcast.place, f32[16,216,128]{2,1,0:T(8,128)S(1)} %all_to_all.11.part_ref), custom_call_target="tpu_custom_call" | custom-call | flops 4000000 | bytes 5000000 | tf_op jit(solution)/shard_map/unpack_first/pallas_call | solution.py:432
  107.0 0.7 collective-permute-done.5.part_ref
  107.7 3.3 %unpack_last.1 = (f32[95,128,128]{2,1,0:T(8,128)}, f32[5,19,128]{2,1,0:T(8,128)}, f32[5,19]{1,0:T(8,128)}) custom-call(s32[1]{0:T(128)} %bitcast.place, f32[16,216,128]{2,1,0:T(8,128)S(1)} %collective-permute-done.5.part_ref, f32[95,128,128]{2,1,0:T(8,128)} %get-tuple-element.13.begun_any, ...), custom_call_target="tpu_custom_call", output_to_operand_aliasing={{0}: (2, {})} | custom-call | flops 4000000 | bytes 5000000 | tf_op jit(solution)/shard_map/unpack_last/pallas_call | solution.py:442
  (1 shorter events, 0.0 us)
Async XLA Ops:
  11.0 11.9 %collective-permute-start = (f32[16,224,128]{2,1,0:T(8,128)S(1)}, f32[16,224,128]{2,1,0:T(8,128)S(1)}, u32[]{:S(2)}, u32[]{:S(2)}) collective-permute-start(f32[16,224,128]{2,1,0:T(8,128)S(1)} %get-tuple-element.12), channel_id=1, source_target_pairs={{0,1},{1,0},{2,3},{3,2},{4,5},{5,4},{6,7},{7,6},{8,9},{9,8},{10,11... | collective-permute-start | bytes 5505032 | tf_op jit(solution)/shard_map/ppermute | solution.py:460
  52.5 17.4 %copy-start = (f32[19,5,128]{2,0,1:T(8,128)S(1)}, f32[19,5,128]{2,0,1:T(8,128)}, u32[]{:S(2)}) copy-start(f32[19,5,128]{2,0,1:T(8,128)} %param.9) | copy-start | bytes 145924
  52.6 9.5 %collective-permute-start.3 = (f32[112,128]{1,0:T(8,128)S(1)}, f32[112,128]{1,0:T(8,128)S(1)}, u32[]{:S(2)}, u32[]{:S(2)}) collective-permute-start(f32[112,128]{1,0:T(8,128)S(1)} %reduce_sum.9), channel_id=1, source_target_pairs={{0,48},{16,0},{32,16},{48,32},{1,49},{17,1},{33,17},{49,33},{2,50}... | collective-permute-start | bytes 172040 | tf_op jit(solution)/shard_map/ppermute | solution.py:466
  58.7 5.1 %collective-permute-start.2 = (f32[112,128]{1,0:T(8,128)S(1)}, f32[112,128]{1,0:T(8,128)S(1)}, u32[]{:S(2)}, u32[]{:S(2)}) collective-permute-start(f32[112,128]{1,0:T(8,128)S(1)} %reduce_sum.9), channel_id=1, source_target_pairs={{0,16},{16,32},{32,48},{48,0},{1,17},{17,33},{33,49},{49,1},{2,18}... | collective-permute-start | bytes 172040 | tf_op jit(solution)/shard_map/ppermute | solution.py:466
  58.7 7.9 %collective-permute-start.1 = (f32[112,128]{1,0:T(8,128)S(1)}, f32[112,128]{1,0:T(8,128)S(1)}, u32[]{:S(2)}, u32[]{:S(2)}) collective-permute-start(f32[112,128]{1,0:T(8,128)S(1)} %reduce_sum.9), channel_id=1, source_target_pairs={{0,32},{16,48},{32,0},{48,16},{1,33},{17,49},{33,1},{49,17},{2,34}... | collective-permute-start | bytes 172040 | tf_op jit(solution)/shard_map/ppermute | solution.py:466
  66.6 3.3 %collective-permute-start.4 = (f32[112,128]{1,0:T(8,128)S(1)}, f32[112,128]{1,0:T(8,128)S(1)}, u32[]{:S(2)}, u32[]{:S(2)}) collective-permute-start(f32[112,128]{1,0:T(8,128)S(1)} %add_add_fusion.mine_ref), channel_id=1, source_target_pairs={{0,8},{8,0},{1,9},{9,1},{2,10},{10,2},{3,11},{11,3},{4,12},{12,4},... | collective-permute-start | bytes 172040 | tf_op jit(solution)/shard_map/ppermute | solution.py:486
  99.3 8.4 %collective-permute-start.5 = (f32[16,216,128]{2,1,0:T(8,128)S(1)}, f32[16,216,128]{2,1,0:T(8,128)S(1)}, u32[]{:S(2)}, u32[]{:S(2)}) collective-permute-start(f32[16,216,128]{2,1,0:T(8,128)S(1)} %all_to_all.11.part_ref), channel_id=1, source_target_pairs={{0,1},{1,0},{2,3},{3,2},{4,5},{5,4},{6,7},{7,6},{8,9},{9,8},{10,11... | collective-permute-start | bytes 5308424 | tf_op jit(solution)/shard_map/ppermute | solution.py:460

commit v7 on v6

--- a/solution.py
+++ b/solution.py
@@ -462,8 +462,8 @@
 
 def sum_far(value):
     total = value
-    for hop in (2, 1, 3):
-        total = total + lax.ppermute(value, "far", [(i, (i + hop) % 4) for i in range(4)])
+    for partners in ((1, 0, 3, 2), (3, 2, 1, 0)):
+        total = total + lax.ppermute(total, "far", list(enumerate(partners)))
     return total
 
 

time: 112 us -> 110 us (0.982)
  starting transfers between devices: 23.3 us -> 20.6 us
  blocking collectives: 52.5 us -> 54 us
    ppermute x3 -> x2, starting transfers between devices: 9.47 us -> 7.02 us  [sum_far(): total = total + lax.ppermute(total, 'far', list(enumerate(partners)))]
    all_to_all x1, blocking collectives: 29.3 us -> 31.7 us  [body(): lax.all_to_all(half.reshape(2 * OWNERS, PART, width), peers, 0, 0, tiled=...]
    ppermute x3 -> x2, waiting for transfers between devices: 4.51 us -> 3.92 us  [sum_far(): total = total + lax.ppermute(total, 'far', list(enumerate(partners)))]
  transfers between devices with their start and end apart: 6 -> 5, of which waited for: 5 -> 5; matrix products, arithmetic and copies ran while one was open for 0% -> 0% of each run, Pallas kernels for 2% -> 2%
where the time goes in v7:
time: 110 us; the launch traced here: 109 us
  blocking collectives  54 us (49%)
  Pallas kernels  22.3 us (20%)
  starting transfers between devices  20.6 us (19%)
  waiting for transfers between devices  11 us (10%)
    all_to_all x1, blocking collectives, body(): lax.all_to_all(half.reshape(2 * OWNERS, PART, width), peers, 0, 0, tiled=...  31.7 us
    all_to_all x1, blocking collectives, body(): here = lax.all_to_all(spread, ('x', 'y'), 0, 0, tiled=True)  22.3 us
    ppermute x2, starting transfers between devices, swap_cores(): return lax.ppermute(value, 'core', [(0, 1), (1, 0)])  13.3 us
    pallas_call x1, Pallas kernels, local_moments(): pl.pallas_call(moments_kernel, in_specs=[smem] + [anywhere] * 6, out_spec...  10.3 us
    ppermute x2, starting transfers between devices, sum_far(): total = total + lax.ppermute(total, 'far', list(enumerate(partners)))  7.02 us
    pallas_call x1, Pallas kernels, solve_share(): pl.pallas_call(solve_kernel, in_specs=[smem, vmem, vmem, vmem], out_specs...  6.08 us
    ppermute x2, waiting for transfers between devices, swap_cores(): return lax.ppermute(value, 'core', [(0, 1), (1, 0)])  4.09 us
    ppermute x2, waiting for transfers between devices, sum_far(): total = total + lax.ppermute(total, 'far', list(enumerate(partners)))  3.92 us
  transfers between devices with their start and end apart: 5, of which 5 were waited for; matrix products, arithmetic and copies ran while one was open for 0% of the time, Pallas kernels for 2%

profile of v7, /device:TPU:1, one launch (start us, length us, event | category | flops | bytes accessed | tf_op | source)
XLA Modules:
  0.0 109.2 jit_solution(2727780686323646543)
XLA Ops:
  0.6 10.3 %moments.1 = (f32[16,224,128]{2,1,0:T(8,128)S(1)}, f32[16,224,128]{2,1,0:T(8,128)S(1)}) custom-call(s32[1]{0:T(128)} %bitcast.place, s32[8,19]{1,0:T(8,128)} %bitcast.19, s32[19]{0:T(128)} %bitcast.21, f32[5,19]{1,0:T(8,128)} %bitcast.20, bf16[32,128,128]{2,1,0:T(8,128)(2,1)} %bitcast.18, bf16[19,5,128,128]{3,2,1,0:T(8,128)(2,1)} %fac_any.1, ...), custom_call_target="tpu_custom_call" | custom-call | tf_op jit(solution)/shard_map/moments/pallas_call | solution.py:228
  11.0 7.2 %collective-permute-start = (f32[16,224,128]{2,1,0:T(8,128)S(1)}, f32[16,224,128]{2,1,0:T(8,128)S(1)}, u32[]{:S(2)}, u32[]{:S(2)}) collective-permute-start(f32[16,224,128]{2,1,0:T(8,128)S(1)} %get-tuple-element.12), channel_id=1, source_target_pairs={{0,1},{1,0},{2,3},{3,2},{4,5},{5,4},{6,7},{7,6},{8,9},{9,8},{10,11... | collective-permute-start | bytes 5505032 | tf_op jit(solution)/shard_map/ppermute | solution.py:460
  18.2 3.4 %collective-permute-done = f32[16,224,128]{2,1,0:T(8,128)S(1)} collective-permute-done((f32[16,224,128]{2,1,0:T(8,128)S(1)}, f32[16,224,128]{2,1,0:T(8,128)S(1)}, u32[]{:S(2)}, u32[]{:S(2)}) %collective-permute-start) | collective-permute-done | bytes 1835040 | tf_op jit(solution)/shard_map/ppermute | solution.py:460
  21.6 0.3 add.17
  21.9 31.7 %all_to_all.10 = f32[32,112,128]{2,1,0:T(8,128)S(1)} all-to-all(f32[32,112,128]{2,1,0:T(8,128)S(1)} %bitcast.16), channel_id=1, replica_groups=mesh['x'=4,'far'=4,'near'=2,'y'=4,'core'=2] {'x','y','near'}, dimensions={0} | all-to-all | bytes 3670016 | tf_op jit(solution)/shard_map/all_to_all | solution.py:483
  53.6 0.0 copy-start
  53.6 0.1 reduce_sum.9
  53.7 3.0 %collective-permute-start.1 = (f32[112,128]{1,0:T(8,128)S(1)}, f32[112,128]{1,0:T(8,128)S(1)}, u32[]{:S(2)}, u32[]{:S(2)}) collective-permute-start(f32[112,128]{1,0:T(8,128)S(1)} %reduce_sum.9), channel_id=1, source_target_pairs={{0,16},{16,0},{32,48},{48,32},{1,17},{17,1},{33,49},{49,33},{2,18}... | collective-permute-start | bytes 172040 | tf_op jit(solution)/shard_map/ppermute | solution.py:466
  56.7 2.2 %collective-permute-done.1 = f32[112,128]{1,0:T(8,128)S(1)} collective-permute-done((f32[112,128]{1,0:T(8,128)S(1)}, f32[112,128]{1,0:T(8,128)S(1)}, u32[]{:S(2)}, u32[]{:S(2)}) %collective-permute-start.1) | collective-permute-done | bytes 57376 | tf_op jit(solution)/shard_map/ppermute | solution.py:466
  58.9 4.0 %collective-permute-start.2 = (f32[112,128]{1,0:T(8,128)S(1)}, f32[112,128]{1,0:T(8,128)S(1)}, u32[]{:S(2)}, u32[]{:S(2)}) collective-permute-start(f32[112,128]{1,0:T(8,128)S(1)} %add.18), channel_id=1, source_target_pairs={{0,48},{16,32},{32,16},{48,0},{1,49},{17,33},{33,17},{49,1},{2,50}... | collective-permute-start | bytes 172040 | tf_op jit(solution)/shard_map/ppermute | solution.py:466
  62.9 1.7 %collective-permute-done.2 = f32[112,128]{1,0:T(8,128)S(1)} collective-permute-done((f32[112,128]{1,0:T(8,128)S(1)}, f32[112,128]{1,0:T(8,128)S(1)}, u32[]{:S(2)}, u32[]{:S(2)}) %collective-permute-start.2) | collective-permute-done | bytes 57376 | tf_op jit(solution)/shard_map/ppermute | solution.py:466
  64.7 0.2 collective-permute-start.3
  64.9 0.1 pad_add_fusion.place
  65.0 3.0 %collective-permute-done.3.theirs_ref = f32[112,128]{1,0:T(8,128)S(1)} collective-permute-done((f32[112,128]{1,0:T(8,128)S(1)}, f32[112,128]{1,0:T(8,128)S(1)}, u32[]{:S(2)}, u32[]{:S(2)}) %collective-permute-start.3) | collective-permute-done | bytes 57376 | tf_op jit(solution)/shard_map/ppermute | solution.py:486
  68.0 0.0 copy-done
  68.0 6.1 %solve.1 = f32[216,128]{1,0:T(8,128)S(1)} custom-call(s32[2]{0:T(128)S(1)} %pad_add_fusion.place, f32[112,128]{1,0:T(8,128)S(1)} %add.19.mine_ref, f32[112,128]{1,0:T(8,128)S(1)} %collective-permute-done.3.theirs_ref, f32[5,19,128]{2,1,0:T(8,128)S(1)} %bitcast.15), custom_call_target="tpu_custom_call" | custom-call | tf_op jit(solution)/shard_map/solve/pallas_call | solution.py:351
  74.1 0.1 broadcast_in_dim.10
  74.2 22.3 %all_to_all.11.part_ref = f32[16,216,128]{2,1,0:T(8,128)S(1)} all-to-all(f32[16,216,128]{2,1,0:T(8,128)S(1)} %broadcast_in_dim.10), channel_id=1, replica_groups=mesh['x'=4,'far'=4,'near'=2,'y'=4,'core'=2] {'x','y'}, dimensions={0} | all-to-all | bytes 3538944 | tf_op jit(solution)/shard_map/all_to_all | solution.py:491
  96.5 6.1 %collective-permute-start.4 = (f32[16,216,128]{2,1,0:T(8,128)S(1)}, f32[16,216,128]{2,1,0:T(8,128)S(1)}, u32[]{:S(2)}, u32[]{:S(2)}) collective-permute-start(f32[16,216,128]{2,1,0:T(8,128)S(1)} %all_to_all.11.part_ref), channel_id=1, source_target_pairs={{0,1},{1,0},{2,3},{3,2},{4,5},{5,4},{6,7},{7,6},{8,9},{9,8},{10,11... | collective-permute-start | bytes 5308424 | tf_op jit(solution)/shard_map/ppermute | solution.py:460
  102.6 2.6 %unpack_first.1 = (f32[95,128,128]{2,1,0:T(8,128)}, f32[5,24,128]{2,1,0:T(8,128)S(1)}, f32[5,24,128]{2,1,0:T(8,128)S(1)}) custom-call(s32[1]{0:T(128)} %bitcast.place, f32[16,216,128]{2,1,0:T(8,128)S(1)} %all_to_all.11.part_ref), custom_call_target="tpu_custom_call" | custom-call | flops 4000000 | bytes 5000000 | tf_op jit(solution)/shard_map/unpack_first/pallas_call | solution.py:432
  105.2 0.7 collective-permute-done.4.part_ref
  105.9 3.3 %unpack_last.1 = (f32[95,128,128]{2,1,0:T(8,128)}, f32[5,19,128]{2,1,0:T(8,128)}, f32[5,19]{1,0:T(8,128)}) custom-call(s32[1]{0:T(128)} %bitcast.place, f32[16,216,128]{2,1,0:T(8,128)S(1)} %collective-permute-done.4.part_ref, f32[95,128,128]{2,1,0:T(8,128)} %get-tuple-element.13.begun_any, ...), custom_call_target="tpu_custom_call", output_to_operand_aliasing={{0}: (2, {})} | custom-call | flops 4000000 | bytes 5000000 | tf_op jit(solution)/shard_map/unpack_last/pallas_call | solution.py:442
  (2 shorter events, 0.0 us)
Async XLA Ops:
  11.0 10.6 %collective-permute-start = (f32[16,224,128]{2,1,0:T(8,128)S(1)}, f32[16,224,128]{2,1,0:T(8,128)S(1)}, u32[]{:S(2)}, u32[]{:S(2)}) collective-permute-start(f32[16,224,128]{2,1,0:T(8,128)S(1)} %get-tuple-element.12), channel_id=1, source_target_pairs={{0,1},{1,0},{2,3},{3,2},{4,5},{5,4},{6,7},{7,6},{8,9},{9,8},{10,11... | collective-permute-start | bytes 5505032 | tf_op jit(solution)/shard_map/ppermute | solution.py:460
  53.6 14.4 %copy-start = (f32[19,5,128]{2,0,1:T(8,128)S(1)}, f32[19,5,128]{2,0,1:T(8,128)}, u32[]{:S(2)}) copy-start(f32[19,5,128]{2,0,1:T(8,128)} %param.9) | copy-start | bytes 145924
  53.7 5.2 %collective-permute-start.1 = (f32[112,128]{1,0:T(8,128)S(1)}, f32[112,128]{1,0:T(8,128)S(1)}, u32[]{:S(2)}, u32[]{:S(2)}) collective-permute-start(f32[112,128]{1,0:T(8,128)S(1)} %reduce_sum.9), channel_id=1, source_target_pairs={{0,16},{16,0},{32,48},{48,32},{1,17},{17,1},{33,49},{49,33},{2,18}... | collective-permute-start | bytes 172040 | tf_op jit(solution)/shard_map/ppermute | solution.py:466
  58.9 5.7 %collective-permute-start.2 = (f32[112,128]{1,0:T(8,128)S(1)}, f32[112,128]{1,0:T(8,128)S(1)}, u32[]{:S(2)}, u32[]{:S(2)}) collective-permute-start(f32[112,128]{1,0:T(8,128)S(1)} %add.18), channel_id=1, source_target_pairs={{0,48},{16,32},{32,16},{48,0},{1,49},{17,33},{33,17},{49,1},{2,50}... | collective-permute-start | bytes 172040 | tf_op jit(solution)/shard_map/ppermute | solution.py:466
  64.7 3.3 %collective-permute-start.3 = (f32[112,128]{1,0:T(8,128)S(1)}, f32[112,128]{1,0:T(8,128)S(1)}, u32[]{:S(2)}, u32[]{:S(2)}) collective-permute-start(f32[112,128]{1,0:T(8,128)S(1)} %add.19.mine_ref), channel_id=1, source_target_pairs={{0,8},{8,0},{1,9},{9,1},{2,10},{10,2},{3,11},{11,3},{4,12},{12,4},... | collective-permute-start | bytes 172040 | tf_op jit(solution)/shard_map/ppermute | solution.py:486
  96.5 9.4 %collective-permute-start.4 = (f32[16,216,128]{2,1,0:T(8,128)S(1)}, f32[16,216,128]{2,1,0:T(8,128)S(1)}, u32[]{:S(2)}, u32[]{:S(2)}) collective-permute-start(f32[16,216,128]{2,1,0:T(8,128)S(1)} %all_to_all.11.part_ref), channel_id=1, source_target_pairs={{0,1},{1,0},{2,3},{3,2},{4,5},{5,4},{6,7},{7,6},{8,9},{9,8},{10,11... | collective-permute-start | bytes 5308424 | tf_op jit(solution)/shard_map/ppermute | solution.py:460
